TPU v7x, 32 devices: a whole 2x2x4 slice. The times are simulated.
32 devices in a mesh: dp: 2 (over x), seq: 16 (over z, y, core).
Axes of the slice: x: 2, y: 2, z: 4, core: 2. Of those that a mesh axis runs over, the one named last changes fastest.
Arguments:
- tokens: bfloat16 [2, 16, 256, 1024], P('dp', 'seq'), may hold values from -24 to 24
- cotangent: bfloat16 [2, 16, 256, 1024], P('dp', 'seq'), may hold values from -6 to 6
- row_mask: int32 [4, 16, 2, 2], P(None, 'seq'), may hold values from 0 to 1, as said below
- column_mask: int32 [4, 256, 2, 2], P(None, 'seq'), may hold values from 0 to 1, as said below
- w_query: bfloat16 [1024, 512], P('dp'), may hold values from -0.25 to 0.25
- w_key: bfloat16 [1024, 512], P('dp'), may hold values from -0.25 to 0.25
- w_value: bfloat16 [1024, 512], P('dp'), may hold values from -0.1875 to 0.1875
- w_out: bfloat16 [512, 1024], P('dp'), may hold values from -0.25 to 0.25
Outputs:
- mixed: bfloat16 [2, 16, 256, 1024], P('dp', 'seq')
- grad_tokens: bfloat16 [2, 16, 256, 1024], P('dp', 'seq')
- grad_value: float32 [1024, 512], P(('dp', 'seq'))
- grad_output: float32 [512, 1024], P(None, ('dp', 'seq'))
Inputs may be any that keep to these rules, and one draw needn't show every extreme that they name: `row_mask`: each block mask is lower triangular with ones on its diagonal. `column_mask`: each block mask is lower triangular with ones on its diagonal.
All inputs are finite; a program needn't handle non-finite values.
Results may differ from a plain program's by a relative error of at most 0.015.
Values may be sent and summed in bfloat16 or wider, within the bound.
A program may use at most 64 MiB of HBM per device.

v0:
```python
import math

import jax
import jax.numpy as jnp
from jax import lax
from jax.sharding import PartitionSpec as P

HEAD_DIM = 64
ROWBLK = 128
COLBLK = 8


row_forms = ("blhe,bmhe->bhlm", "bhlm,bmhe->blhe")
column_forms = ("lbhe,mbhe->bhlm", "bhlm,mbhe->lbhe")
contract_last = (((1,), (1,)), ((), ()))
contract_first = (((0,), (0,)), ((), ()))


def allowed_cells(mask_blocks, block_size):
    expanded = jnp.repeat(jnp.repeat(mask_blocks, block_size, axis=-2), block_size, axis=-1)
    length = expanded.shape[-1]
    causal = jnp.arange(length)[:, None] >= jnp.arange(length)[None, :]
    return (expanded == 1) & causal


def attend(queries, key_part, value_part, allowed, forms):
    scale_factor = 1.0 / math.sqrt(queries.shape[-1])
    scores = (
        jnp.einsum(forms[0], queries.astype(jnp.float32), key_part.astype(jnp.float32))
        * scale_factor
    )
    scores = jnp.where(allowed, scores, -1e30)
    highest = lax.stop_gradient(jnp.max(scores, axis=-1, keepdims=True))
    weights = jnp.exp(scores - highest)
    weights = weights / jnp.sum(weights, axis=-1, keepdims=True)
    rounded = lax.optimization_barrier(weights.astype(jnp.bfloat16)).astype(jnp.float32)
    result = jnp.einsum(forms[1], rounded, value_part.astype(jnp.float32))
    return result.astype(jnp.bfloat16)


def body(tokens, cotangent, row_mask, column_mask, w_query, w_key, w_value, w_out):
    rows_here = tokens.shape[1]
    grid_cols = tokens.shape[2]
    width = tokens.shape[3]
    heads_width = w_query.shape[1]
    half = heads_width // HEAD_DIM // 2
    split = half * HEAD_DIM
    flat = tokens.reshape(-1, width)
    cot_flat = cotangent.reshape(-1, width)
    token_count = flat.shape[0]
    seq_count = lax.axis_size("seq")
    grid_rows = rows_here * seq_count
    cols_here = grid_cols // seq_count
    full_query, full_key, full_value, full_out = (
        lax.all_gather(w_query, "dp", axis=0, tiled=True),
        lax.all_gather(w_key, "dp", axis=0, tiled=True),
        lax.all_gather(w_value, "dp", axis=0, tiled=True),
        lax.all_gather(w_out, "dp", axis=0, tiled=True),
    )
    proj_query = jnp.dot(flat, full_query, preferred_element_type=jnp.float32)
    proj_key = jnp.dot(flat, full_key, preferred_element_type=jnp.float32)
    proj_value = jnp.dot(flat, full_value, preferred_element_type=jnp.float32)
    query_flat = proj_query.astype(jnp.bfloat16)
    key_flat = proj_key.astype(jnp.bfloat16)
    value_flat = proj_value.astype(jnp.bfloat16)
    row_allowed = allowed_cells(jnp.transpose(row_mask, (1, 0, 2, 3)), ROWBLK)
    column_allowed = allowed_cells(jnp.transpose(column_mask, (1, 0, 2, 3)), COLBLK)

    def row_core(first, second, third):
        return attend(first, second, third, row_allowed, row_forms)

    def column_core(first, second, third):
        return attend(first, second, third, column_allowed, column_forms)

    def row_heads(matrix):
        return matrix[:, :split].reshape(rows_here, grid_cols, half, HEAD_DIM)

    def column_heads(matrix):
        return matrix[:, split:].reshape(rows_here, grid_cols, split)

    def as_columns(block):
        return block.reshape(grid_rows, cols_here, half, HEAD_DIM)

    def joined(row_part, col_part):
        return jnp.concatenate(
            [row_part.reshape(token_count, split), col_part.reshape(token_count, split)], axis=1
        )

    col_query, col_key, col_value = (
        lax.all_to_all(column_heads(query_flat), "seq", split_axis=1, concat_axis=0, tiled=True),
        lax.all_to_all(column_heads(key_flat), "seq", split_axis=1, concat_axis=0, tiled=True),
        lax.all_to_all(column_heads(value_flat), "seq", split_axis=1, concat_axis=0, tiled=True),
    )
    row_out, row_back = jax.vjp(
        row_core, row_heads(query_flat), row_heads(key_flat), row_heads(value_flat)
    )
    column_out, column_back = jax.vjp(
        column_core, as_columns(col_query), as_columns(col_key), as_columns(col_value)
    )
    returned = lax.all_to_all(
        column_out.reshape(grid_rows, cols_here, split),
        "seq",
        split_axis=0,
        concat_axis=1,
        tiled=True,
    )
    attended = joined(row_out, returned)
    mixed = jnp.dot(attended, full_out, preferred_element_type=jnp.float32)
    grad_heads = lax.dot_general(
        cot_flat, full_out, contract_last, preferred_element_type=jnp.float32
    )
    mixed = mixed.astype(jnp.bfloat16).reshape(tokens.shape)
    grad_heads = grad_heads.astype(jnp.bfloat16)
    row_grads = row_back(grad_heads[:, :split].reshape(rows_here, grid_cols, half, HEAD_DIM))
    grad_columns = lax.all_to_all(
        grad_heads[:, split:].reshape(rows_here, grid_cols, split),
        "seq",
        split_axis=1,
        concat_axis=0,
        tiled=True,
    )
    col_grads = column_back(as_columns(grad_columns))
    back_grads = (
        lax.all_to_all(
            col_grads[0].reshape(grid_rows, cols_here, split),
            "seq",
            split_axis=0,
            concat_axis=1,
            tiled=True,
        ),
        lax.all_to_all(
            col_grads[1].reshape(grid_rows, cols_here, split),
            "seq",
            split_axis=0,
            concat_axis=1,
            tiled=True,
        ),
        lax.all_to_all(
            col_grads[2].reshape(grid_rows, cols_here, split),
            "seq",
            split_axis=0,
            concat_axis=1,
            tiled=True,
        ),
    )
    grad_query = joined(row_grads[0], back_grads[0])
    grad_key = joined(row_grads[1], back_grads[1])
    grad_val = joined(row_grads[2], back_grads[2])
    grad_tokens = (
        lax.dot_general(grad_query, full_query, contract_last, preferred_element_type=jnp.float32)
        + lax.dot_general(grad_key, full_key, contract_last, preferred_element_type=jnp.float32)
        + lax.dot_general(grad_val, full_value, contract_last, preferred_element_type=jnp.float32)
    )
    grad_tokens = grad_tokens.astype(jnp.bfloat16).reshape(tokens.shape)
    summed = lax.psum_scatter(
        jnp.concatenate(
            [
                lax.dot_general(flat, grad_val, contract_first, preferred_element_type=jnp.float32),
                lax.dot_general(
                    cot_flat, attended, contract_first, preferred_element_type=jnp.float32
                ),
            ],
            axis=1,
        ),
        ("dp", "seq"),
        scatter_dimension=0,
        tiled=True,
    )
    grad_value = summed[:, :heads_width]
    grad_output = jnp.transpose(summed[:, heads_width:])
    return (mixed, grad_tokens, grad_value, grad_output)


def solution(mesh):
    return jax.shard_map(
        body,
        mesh=mesh,
        in_specs=(
            P("dp", "seq", None, None),
            P("dp", "seq", None, None),
            P(None, "seq", None, None),
            P(None, "seq", None, None),
            P("dp", None),
            P("dp", None),
            P("dp", None),
            P("dp", None),
        ),
        out_specs=(
            P("dp", "seq", None, None),
            P("dp", "seq", None, None),
            P(("dp", "seq"), None),
            P(None, ("dp", "seq")),
        ),
        check_vma=False,
    )
```

profile of v0, /device:TPU:0, one launch (start us, length us, event | category | flops | bytes accessed | tf_op | source)
XLA Modules:
  0.0 332.4 jit_solution(15236379974072211700)
XLA Ops:
  11.3 22.4 %all-gather.11.cloned.1.call-done = bf16[512,1024]{1,0:T(8,128)(2,1)} async-done(((bf16[256,1024]{1,0:T(8,128)(2,1)}), bf16[512,1024]{1,0:T(8,128)(2,1)}) %all-gather.11.cloned.1.call-update) | async-done | bytes 1048592 | tf_op jit(solution)/shard_map/all_gather | solution.py:58
  33.6 1.7 convolution_convert_fusion.6
  38.2 5.6 %all-to-all-start.4 = ((bf16[16,2,2048]{2,1,0:T(2,128)(2,1)}), bf16[16,2,2048]{2,1,0:T(2,128)(2,1)S(1)}, u32[]{:S(2)}, u32[]{:S(2)}) async-start(bf16[16,2,2048]{2,1,0:T(2,128)(2,1)} %reshape.321), calls=%async_computation.4 | async-start | bytes 262144 | tf_op jit(solution)/shard_map/all_to_all | solution.py:115
  43.9 12.7 %all-gather.5.cloned.1.call-done = bf16[1024,512]{1,0:T(8,128)(2,1)} async-done(((bf16[512,512]{1,0:T(8,128)(2,1)}), bf16[1024,512]{1,0:T(8,128)(2,1)}) %all-gather.5.cloned.1.call-update) | async-done | bytes 1048592 | tf_op jit(solution)/shard_map/all_gather | solution.py:57
  56.5 1.7 convolution_convert_fusion.10
  60.5 18.9 %all-gather.9.cloned.1.call-done = bf16[1024,512]{1,0:T(8,128)(2,1)} async-done(((bf16[512,512]{1,0:T(8,128)(2,1)}), bf16[1024,512]{1,0:T(8,128)(2,1)}) %all-gather.9.cloned.1.call-update) | async-done | bytes 1048592 | tf_op jit(solution)/shard_map/all_gather | solution.py:56
  79.4 1.7 convolution_convert_fusion.8
  81.2 20.9 %all-gather.7.cloned.1.call-done = bf16[1024,512]{1,0:T(8,128)(2,1)} async-done(((bf16[512,512]{1,0:T(8,128)(2,1)}), bf16[1024,512]{1,0:T(8,128)(2,1)}) %all-gather.7.cloned.1.call-update) | async-done | bytes 1048592 | tf_op jit(solution)/shard_map/all_gather | solution.py:55
  102.1 1.7 convolution_convert_fusion.9
  105.2 5.6 %all-to-all-start = ((bf16[16,2,2048]{2,1,0:T(2,128)(2,1)}), bf16[16,2,2048]{2,1,0:T(2,128)(2,1)S(1)}, u32[]{:S(2)}, u32[]{:S(2)}) async-start(bf16[16,2,2048]{2,1,0:T(2,128)(2,1)} %reshape.319), calls=%async_computation | async-start | bytes 262144 | tf_op jit(solution)/shard_map/all_to_all | solution.py:92
  118.8 5.0 %all-to-all-start.2 = ((bf16[16,2,2048]{2,1,0:T(2,128)(2,1)}), bf16[16,2,2048]{2,1,0:T(2,128)(2,1)}, u32[]{:S(2)}, u32[]{:S(2)}) async-start(bf16[16,2,2048]{2,1,0:T(2,128)(2,1)} %reshape.315), calls=%async_computation.2 | async-start | bytes 262144 | tf_op jit(solution)/shard_map/all_to_all | solution.py:91
  125.8 6.0 %all-to-all-done.2 = bf16[16,2,2048]{2,1,0:T(2,128)(2,1)} async-done(((bf16[16,2,2048]{2,1,0:T(2,128)(2,1)}), bf16[16,2,2048]{2,1,0:T(2,128)(2,1)}, u32[]{:S(2)}, u32[]{:S(2)}) %all-to-all-start.2) | async-done | bytes 131104 | tf_op jit(solution)/shard_map/all_to_all | solution.py:91
  131.8 4.3 %all-to-all-start.1 = ((bf16[16,2,2048]{2,1,0:T(2,128)(2,1)}), bf16[16,2,2048]{2,1,0:T(2,128)(2,1)}, u32[]{:S(2)}, u32[]{:S(2)}) async-start(bf16[16,2,2048]{2,1,0:T(2,128)(2,1)} %reshape.317), calls=%async_computation.1 | async-start | bytes 262144 | tf_op jit(solution)/shard_map/all_to_all | solution.py:90
  140.1 1.8 reshape.289
  141.8 2.1 all-to-all-done.1
  149.3 2.1 fusion.70
  153.6 3.7 %all-to-all-start.7 = ((bf16[16,16,256]{2,1,0:T(8,128)(2,1)}), bf16[16,16,256]{2,1,0:T(8,128)(2,1)S(1)}, u32[]{:S(2)}, u32[]{:S(2)}) async-start(bf16[16,16,256]{2,1,0:T(8,128)(2,1)} %reshape.306), calls=%async_computation.7 | async-start | bytes 262144 | tf_op jit(solution)/shard_map/all_to_all | solution.py:138
  159.9 5.3 %all-to-all-done.7 = bf16[16,16,256]{2,1,0:T(8,128)(2,1)S(1)} async-done(((bf16[16,16,256]{2,1,0:T(8,128)(2,1)}), bf16[16,16,256]{2,1,0:T(8,128)(2,1)S(1)}, u32[]{:S(2)}, u32[]{:S(2)}) %all-to-all-start.7) | async-done | bytes 131104 | tf_op jit(solution)/shard_map/all_to_all | solution.py:138
  165.2 3.5 %all-to-all-start.3 = ((bf16[16,16,256]{2,1,0:T(8,128)(2,1)}), bf16[16,16,256]{2,1,0:T(8,128)(2,1)S(1)}, u32[]{:S(2)}, u32[]{:S(2)}) async-start(bf16[16,16,256]{2,1,0:T(8,128)(2,1)} %reshape.290), calls=%async_computation.3 | async-start | bytes 262144 | tf_op jit(solution)/shard_map/all_to_all | solution.py:100
  168.8 1.8 convolution_bitcast_fusion.1
  170.6 6.1 %all-to-all-done.3 = bf16[16,16,256]{2,1,0:T(8,128)(2,1)S(1)} async-done(((bf16[16,16,256]{2,1,0:T(8,128)(2,1)}), bf16[16,16,256]{2,1,0:T(8,128)(2,1)S(1)}, u32[]{:S(2)}, u32[]{:S(2)}) %all-to-all-start.3) | async-done | bytes 131104 | tf_op jit(solution)/shard_map/all_to_all | solution.py:100
  178.2 2.5 pad_maximum_fusion
  180.7 5.3 %copy.152 = f32[1024,1024]{1,0:T(8,128)} copy(f32[1024,1024]{0,1:T(8,128)} %pad_maximum_fusion) | data formatting | bytes 8388608
  191.2 1.6 fusion.13
  193.8 3.5 %all-to-all-start.5 = ((bf16[16,16,256]{2,1,0:T(8,128)(2,1)}), bf16[16,16,256]{2,1,0:T(8,128)(2,1)S(1)}, u32[]{:S(2)}, u32[]{:S(2)}) async-start(bf16[16,16,256]{2,1,0:T(8,128)(2,1)} %reshape.300), calls=%async_computation.5 | async-start | bytes 262144 | tf_op jit(solution)/shard_map/all_to_all | solution.py:124
  197.3 2.1 fusion.14
  202.6 2.9 all-to-all-done.5
  205.5 3.5 %all-to-all-start.6 = ((bf16[16,16,256]{2,1,0:T(8,128)(2,1)}), bf16[16,16,256]{2,1,0:T(8,128)(2,1)S(1)}, u32[]{:S(2)}, u32[]{:S(2)}) async-start(bf16[16,16,256]{2,1,0:T(8,128)(2,1)} %reshape.303), calls=%async_computation.6 | async-start | bytes 262144 | tf_op jit(solution)/shard_map/all_to_all | solution.py:131
  209.0 1.7 fusion.38
  210.7 6.5 %all-to-all-done.6 = bf16[16,16,256]{2,1,0:T(8,128)(2,1)S(1)} async-done(((bf16[16,16,256]{2,1,0:T(8,128)(2,1)}), bf16[16,16,256]{2,1,0:T(8,128)(2,1)S(1)}, u32[]{:S(2)}, u32[]{:S(2)}) %all-to-all-start.6) | async-done | bytes 131104 | tf_op jit(solution)/shard_map/all_to_all | solution.py:131
  219.7 104.6 %reduce-scatter.4.cloned.1.call-done = f32[32,1024]{1,0:T(8,128)} async-done(((f32[1024,1024]{1,0:T(8,128)}), f32[32,1024]{1,0:T(8,128)}) %reduce-scatter.4.cloned.1.call-update) | async-done | bytes 131088
  324.3 1.5 slice_bitcast_fusion.4
  (158 shorter events, 47.6 us)
Async XLA Ops:
  7.2 49.3 %copy-start = (bf16[1,1,256,1024]{3,2,1,0:T(8,128)(2,1)S(1)}, bf16[1,1,256,1024]{3,2,1,0:T(8,128)(2,1)}, u32[]{:S(2)}) copy-start(bf16[1,1,256,1024]{3,2,1,0:T(8,128)(2,1)} %param.8) | copy-start | bytes 1572868
  7.2 26.4 %copy-start.5 = (bf16[1,1,256,1024]{3,2,1,0:T(8,128)(2,1)S(1)}, bf16[1,1,256,1024]{3,2,1,0:T(8,128)(2,1)}, u32[]{:S(2)}) copy-start(bf16[1,1,256,1024]{3,2,1,0:T(8,128)(2,1)} %param.9) | copy-start | bytes 1572868
  7.2 26.4 %all-gather.11.cloned.1.call-start = ((), (), s32[]{:S(2)}) async-start(), calls=%async_computation.12 | async-start | bytes 1572864 | tf_op jit(solution)/shard_map/all_gather | solution.py:58
  7.9 48.6 %all-gather.5.cloned.1.call-start = ((), (), s32[]{:S(2)}) async-start(), calls=%async_computation.9 | async-start | bytes 1572864 | tf_op jit(solution)/shard_map/all_gather | solution.py:57
  8.7 70.7 %all-gather.9.cloned.1.call-start = ((), (), s32[]{:S(2)}) async-start(), calls=%async_computation.11 | async-start | bytes 1572864 | tf_op jit(solution)/shard_map/all_gather | solution.py:56
  9.4 92.7 %all-gather.7.cloned.1.call-start = ((), (), s32[]{:S(2)}) async-start(), calls=%async_computation.10 | async-start | bytes 1572864 | tf_op jit(solution)/shard_map/all_gather | solution.py:55
  10.1 25.3 %copy-start.16 = (pred[256,256]{0,1:T(8,128)(4,1)}, pred[256,256]{0,1:T(8,128)(4,1)S(1)}, u32[]{:S(2)}) copy-start(pred[256,256]{0,1:T(8,128)(4,1)S(1)} %iota_compare_fusion) | copy-start | bytes 196612
  38.2 66.9 %all-to-all-start.4 = ((bf16[16,2,2048]{2,1,0:T(2,128)(2,1)}), bf16[16,2,2048]{2,1,0:T(2,128)(2,1)S(1)}, u32[]{:S(2)}, u32[]{:S(2)}) async-start(bf16[16,2,2048]{2,1,0:T(2,128)(2,1)} %reshape.321), calls=%async_computation.4 | async-start | bytes 262144 | tf_op jit(solution)/shard_map/all_to_all | solution.py:115
  81.2 24.0 %copy-start.21 = (bf16[256,256]{0,1:T(8,128)(2,1)}, bf16[256,256]{0,1:T(8,128)(2,1)S(1)}, u32[]{:S(2)}) copy-start(bf16[256,256]{0,1:T(8,128)(2,1)S(1)} %copy.109) | copy-start | bytes 393220
  104.6 6.2 %copy-start.23 = (bf16[256,256]{0,1:T(8,128)(2,1)}, bf16[256,256]{0,1:T(8,128)(2,1)S(1)}, u32[]{:S(2)}) copy-start(bf16[256,256]{0,1:T(8,128)(2,1)S(1)} %copy.108) | copy-start | bytes 393220
  105.2 13.6 %all-to-all-start = ((bf16[16,2,2048]{2,1,0:T(2,128)(2,1)}), bf16[16,2,2048]{2,1,0:T(2,128)(2,1)S(1)}, u32[]{:S(2)}, u32[]{:S(2)}) async-start(bf16[16,2,2048]{2,1,0:T(2,128)(2,1)} %reshape.319), calls=%async_computation | async-start | bytes 262144 | tf_op jit(solution)/shard_map/all_to_all | solution.py:92
  111.0 13.5 %copy-start.10 = (bf16[256,256]{0,1:T(8,128)(2,1)}, bf16[256,256]{0,1:T(8,128)(2,1)S(1)}, u32[]{:S(2)}) copy-start(bf16[256,256]{0,1:T(8,128)(2,1)S(1)} %copy.122) | copy-start | bytes 393220
  111.1 46.1 %copy-start.12 = (bf16[256,256]{0,1:T(8,128)(2,1)}, bf16[256,256]{0,1:T(8,128)(2,1)S(1)}, u32[]{:S(2)}) copy-start(bf16[256,256]{0,1:T(8,128)(2,1)S(1)} %copy.104) | copy-start | bytes 393220
  118.8 13.0 %all-to-all-start.2 = ((bf16[16,2,2048]{2,1,0:T(2,128)(2,1)}), bf16[16,2,2048]{2,1,0:T(2,128)(2,1)}, u32[]{:S(2)}, u32[]{:S(2)}) async-start(bf16[16,2,2048]{2,1,0:T(2,128)(2,1)} %reshape.315), calls=%async_computation.2 | async-start | bytes 262144 | tf_op jit(solution)/shard_map/all_to_all | solution.py:91
  131.8 12.1 %all-to-all-start.1 = ((bf16[16,2,2048]{2,1,0:T(2,128)(2,1)}), bf16[16,2,2048]{2,1,0:T(2,128)(2,1)}, u32[]{:S(2)}, u32[]{:S(2)}) async-start(bf16[16,2,2048]{2,1,0:T(2,128)(2,1)} %reshape.317), calls=%async_computation.1 | async-start | bytes 262144 | tf_op jit(solution)/shard_map/all_to_all | solution.py:90
  147.7 3.7 %copy-start.28 = (bf16[16,16,4,64]{3,2,1,0:T(4,128)(2,1)}, bf16[16,16,4,64]{3,2,1,0:T(4,128)(2,1)S(1)}, u32[]{:S(2)}) copy-start(bf16[16,16,4,64]{3,2,1,0:T(4,128)(2,1)S(1)} %reshape.287) | copy-start | bytes 393220
  147.8 3.7 %copy-start.14 = (bf16[16,4,16,16]{2,3,1,0:T(8,128)(2,1)S(1)}, bf16[16,4,16,16]{2,3,1,0:T(8,128)(2,1)}, u32[]{:S(2)}) copy-start(bf16[16,4,16,16]{2,3,1,0:T(8,128)(2,1)} %convolution_convert_fusion.5) | copy-start | bytes 98308
  153.6 11.6 %all-to-all-start.7 = ((bf16[16,16,256]{2,1,0:T(8,128)(2,1)}), bf16[16,16,256]{2,1,0:T(8,128)(2,1)S(1)}, u32[]{:S(2)}, u32[]{:S(2)}) async-start(bf16[16,16,256]{2,1,0:T(8,128)(2,1)} %reshape.306), calls=%async_computation.7 | async-start | bytes 262144 | tf_op jit(solution)/shard_map/all_to_all | solution.py:138
  158.6 12.0 %copy-start.8 = (bf16[256,256]{1,0:T(8,128)(2,1)}, bf16[256,256]{1,0:T(8,128)(2,1)S(1)}, u32[]{:S(2)}) copy-start(bf16[256,256]{1,0:T(8,128)(2,1)S(1)} %copy.139) | copy-start | bytes 393220
  165.2 11.9 %copy-start.6 = (bf16[16,16,256]{2,1,0:T(8,128)(2,1)}, bf16[16,16,256]{2,1,0:T(8,128)(2,1)S(1)}, u32[]{:S(2)}) copy-start(bf16[16,16,256]{2,1,0:T(8,128)(2,1)S(1)} %all-to-all-done.7) | copy-start | bytes 393220
  165.2 11.4 %all-to-all-start.3 = ((bf16[16,16,256]{2,1,0:T(8,128)(2,1)}), bf16[16,16,256]{2,1,0:T(8,128)(2,1)S(1)}, u32[]{:S(2)}, u32[]{:S(2)}) async-start(bf16[16,16,256]{2,1,0:T(8,128)(2,1)} %reshape.290), calls=%async_computation.3 | async-start | bytes 262144 | tf_op jit(solution)/shard_map/all_to_all | solution.py:100
  168.7 155.6 %reduce-scatter.4.cloned.1.call-start = ((), (), s32[]{:S(2)}) async-start(), calls=%async_computation.13 | async-start | bytes 4325376
  191.2 6.1 %copy-start.20 = (f32[16,4,16,16]{2,3,1,0:T(8,128)S(1)}, f32[16,4,16,16]{2,3,1,0:T(8,128)}, u32[]{:S(2)}) copy-start(f32[16,4,16,16]{2,3,1,0:T(8,128)} %copy-done.18) | copy-start | bytes 196612
  191.2 6.2 %copy-start.27 = (f32[16,4,16]{2,1,0:T(4,128)S(1)}, f32[16,4,16]{2,1,0:T(4,128)}, u32[]{:S(2)}) copy-start(f32[16,4,16]{2,1,0:T(4,128)} %copy-done.25) | copy-start | bytes 12292
  191.2 6.2 %copy-start.29 = (bf16[16,16,4,64]{3,2,1,0:T(4,128)(2,1)S(1)}, bf16[16,16,4,64]{3,2,1,0:T(4,128)(2,1)}, u32[]{:S(2)}) copy-start(bf16[16,16,4,64]{3,2,1,0:T(4,128)(2,1)} %copy-done.28) | copy-start | bytes 393220
  193.8 11.7 %all-to-all-start.5 = ((bf16[16,16,256]{2,1,0:T(8,128)(2,1)}), bf16[16,16,256]{2,1,0:T(8,128)(2,1)S(1)}, u32[]{:S(2)}, u32[]{:S(2)}) async-start(bf16[16,16,256]{2,1,0:T(8,128)(2,1)} %reshape.300), calls=%async_computation.5 | async-start | bytes 262144 | tf_op jit(solution)/shard_map/all_to_all | solution.py:124
  197.3 4.0 %copy-start.2 = (bf16[512,1024]{1,0:T(8,128)(2,1)S(1)}, bf16[512,1024]{1,0:T(8,128)(2,1)}, u32[]{:S(2)}) copy-start(bf16[512,1024]{1,0:T(8,128)(2,1)} %all-gather.11.cloned.1.call-done) | copy-start | bytes 3145732
  201.4 15.8 %copy-start.3 = (bf16[1024,512]{1,0:T(8,128)(2,1)S(1)}, bf16[1024,512]{1,0:T(8,128)(2,1)}, u32[]{:S(2)}) copy-start(bf16[1024,512]{1,0:T(8,128)(2,1)} %all-gather.9.cloned.1.call-done) | copy-start | bytes 3145732
  201.4 15.8 %copy-start.24 = (bf16[256,256]{1,0:T(8,128)(2,1)S(1)}, bf16[256,256]{1,0:T(8,128)(2,1)}, u32[]{:S(2)}) copy-start(bf16[256,256]{1,0:T(8,128)(2,1)} %copy.136) | copy-start | bytes 393220
  205.5 11.7 %all-to-all-start.6 = ((bf16[16,16,256]{2,1,0:T(8,128)(2,1)}), bf16[16,16,256]{2,1,0:T(8,128)(2,1)S(1)}, u32[]{:S(2)}, u32[]{:S(2)}) async-start(bf16[16,16,256]{2,1,0:T(8,128)(2,1)} %reshape.303), calls=%async_computation.6 | async-start | bytes 262144 | tf_op jit(solution)/shard_map/all_to_all | solution.py:131
  210.7 7.0 %copy-start.7 = (bf16[16,16,256]{2,1,0:T(8,128)(2,1)S(1)}, bf16[16,16,256]{2,1,0:T(8,128)(2,1)}, u32[]{:S(2)}) copy-start(bf16[16,16,256]{2,1,0:T(8,128)(2,1)} %copy-done.6) | copy-start | bytes 393220
  210.7 7.0 %copy-start.9 = (bf16[256,256]{1,0:T(8,128)(2,1)S(1)}, bf16[256,256]{1,0:T(8,128)(2,1)}, u32[]{:S(2)}) copy-start(bf16[256,256]{1,0:T(8,128)(2,1)} %copy-done.8) | copy-start | bytes 393220
  (15 other events, 29.1 us)
Sparse Core Ops, SparseCore 0:
  9.6 23.9 all-gather.10
  35.2 21.2 all-gather.4
  58.1 21.2 all-gather.8
  80.8 21.2 all-gather.6
  186.2 138.0 reduce-scatter.3
where the time goes:
time: 334 us; the launch traced here: 332 us
  waiting for transfers between devices  212 us (63%)
  local copies, waits for them, and re-layouts  35.2 us (11%)
  starting transfers between devices  35 us (10%)
  matrix products  23.9 us (7%)
  between operations  14.6 us (4%)
  other arithmetic  11.8 us (4%)
    unnamed x6, waiting for transfers between devices  107 us
    all_gather x1, waiting for transfers between devices, body(): lax.all_gather(w_out, 'dp', axis=0, tiled=True)  22.4 us
    all_gather x1, waiting for transfers between devices, body(): lax.all_gather(w_query, 'dp', axis=0, tiled=True)  20.9 us
    all_gather x1, waiting for transfers between devices, body(): lax.all_gather(w_key, 'dp', axis=0, tiled=True)  18.9 us
    unnamed x78, local copies, waits for them, and re-layouts  15.5 us
    all_gather x1, waiting for transfers between devices, body(): lax.all_gather(w_value, 'dp', axis=0, tiled=True)  12.7 us
  transfers between devices with their start and end apart: 13, of which 12 were waited for; matrix products, arithmetic and copies ran while one was open for 14% of the time, Pallas kernels for 0%

commit v1 on v0

--- a/solution.py
+++ b/solution.py
@@ -3,6 +3,8 @@
 import jax
 import jax.numpy as jnp
 from jax import lax
+from jax.experimental import pallas as pl
+from jax.experimental.pallas import tpu as pltpu
 from jax.sharding import PartitionSpec as P
 
 HEAD_DIM = 64
@@ -171,9 +173,459 @@
     return (mixed, grad_tokens, grad_value, grad_output)
 
 
+MESH = pl.DeviceIdType.MESH
+F32 = jnp.float32
+BF16 = jnp.bfloat16
+
+
+def dot_nn(a, b):
+    return jnp.dot(a, b, preferred_element_type=F32)
+
+
+def dot_nt(a, b):
+    return lax.dot_general(a, b, contract_last, preferred_element_type=F32)
+
+
+def dot_tn(a, b):
+    return lax.dot_general(a, b, contract_first, preferred_element_type=F32)
+
+
+def fused_kernel(
+    dp_count,
+    seq_count,
+    tokens_ref,
+    cot_ref,
+    bits_ref,
+    wq_ref,
+    wk_ref,
+    wv_ref,
+    wo_ref,
+    mixed_ref,
+    gtok_ref,
+    gval_ref,
+    gout_ref,
+    w_full,
+    wo_full,
+    qkv_send,
+    qkv_recv,
+    g_rows,
+    g_send,
+    g_recv,
+    out_send,
+    out_recv,
+    grad_send,
+    grad_recv,
+    row_grads,
+    probs,
+    attended,
+    part,
+    part_recv1,
+    acc1,
+    part_recv2,
+    acc2,
+    part_recv3,
+    acc3,
+    part_recv4,
+    w_send_sem,
+    w_recv_sem,
+    a_send_sem,
+    a_recv_sem,
+    r_send_sem,
+    r_recv_sem,
+):
+    dp = lax.axis_index("dp")
+    seq = lax.axis_index("seq")
+    core = lax.rem(seq, 2)
+    y = lax.rem(seq // 2, 2)
+    z = seq // 4
+    z_count = seq_count // 4
+    positions = tokens_ref.shape[0]
+    cols = positions // seq_count
+    shard = wq_ref.shape[0]
+    out_shard = wo_ref.shape[0]
+    split = qkv_send.shape[2]
+    other = 1 - dp
+    x_peer = (other, seq)
+    core_peer = (dp, seq + 1 - 2 * core)
+    y_peer = (dp, seq + 2 - 4 * y)
+
+    barrier = pltpu.get_barrier_semaphore()
+    pl.semaphore_signal(barrier, inc=1, device_id=x_peer, device_id_type=MESH)
+
+    @pl.loop(1, seq_count)
+    def _(step):
+        pl.semaphore_signal(
+            barrier,
+            inc=1,
+            device_id=(dp, lax.rem(seq + step, seq_count)),
+            device_id_type=MESH,
+        )
+
+    own_rows = pl.ds(pl.multiple_of(dp * shard, shard), shard)
+    w_full[0, own_rows, :] = wq_ref[...]
+    w_full[1, own_rows, :] = wk_ref[...]
+    w_full[2, own_rows, :] = wv_ref[...]
+    own_out = pl.ds(pl.multiple_of(dp * out_shard, out_shard), out_shard)
+    wo_full[own_out, :] = wo_ref[...]
+    pl.semaphore_wait(barrier, seq_count)
+
+    def region(group, owner, qy, qc):
+        if group == 1:
+            quarter = out_shard // 4
+            start = pl.multiple_of(owner * out_shard + (qy * 2 + qc) * quarter, quarter)
+            return wo_full.at[pl.ds(start, quarter), :]
+        quarter = shard // 4
+        start = pl.multiple_of(owner * shard + (qy * 2 + qc) * quarter, quarter)
+        lanes = pl.ds(split if group == 0 else 0, split)
+        return w_full.at[:, pl.ds(start, quarter), lanes]
+
+    def weight_copy(group, hop):
+        if hop == 0:
+            ref, peer = region(group, dp, y, core), x_peer
+        elif hop == 1:
+            ref, peer = region(group, other, y, core), y_peer
+        elif hop == 2:
+            ref, peer = region(group, other, y, core), core_peer
+        else:
+            ref, peer = region(group, other, 1 - y, core), core_peer
+        return pltpu.make_async_remote_copy(
+            src_ref=ref,
+            dst_ref=ref,
+            send_sem=w_send_sem.at[group, hop],
+            recv_sem=w_recv_sem.at[group, hop],
+            device_id=peer,
+            device_id_type=MESH,
+        )
+
+    def share_weights(group):
+        weight_copy(group, 0).wait_recv()
+        if group < 2:
+            weight_copy(group + 1, 0).start()
+        weight_copy(group, 1).start()
+        weight_copy(group, 2).start()
+        weight_copy(group, 1).wait_recv()
+        weight_copy(group, 3).start()
+        weight_copy(group, 2).wait_recv()
+        weight_copy(group, 3).wait_recv()
+
+    def column_copy(src, dst, phase, step):
+        target = lax.rem(seq + step, seq_count)
+        there = pl.ds(pl.multiple_of(target * cols, cols), cols)
+        here = pl.ds(pl.multiple_of(seq * cols, cols), cols)
+        return pltpu.make_async_remote_copy(
+            src_ref=src.at[:, there, :],
+            dst_ref=dst.at[:, here, :],
+            send_sem=a_send_sem.at[phase, step],
+            recv_sem=a_recv_sem.at[phase, step],
+            device_id=(dp, target),
+            device_id_type=MESH,
+        )
+
+    def exchange(src, dst, phase):
+        @pl.loop(1, seq_count)
+        def _(step):
+            column_copy(src, dst, phase, step).start()
+
+        here = pl.ds(pl.multiple_of(seq * cols, cols), cols)
+        dst[:, here, :] = src[:, here, :]
+
+    def arrived(src, dst, phase):
+        @pl.loop(1, seq_count)
+        def _(step):
+            column_copy(src, dst, phase, step).wait_recv()
+
+    def sent(src, dst, phase):
+        @pl.loop(1, seq_count)
+        def _(step):
+            column_copy(src, dst, phase, step).wait_send()
+
+    weight_copy(0, 0).start()
+
+    query_pos = lax.broadcasted_iota(jnp.int32, (positions, positions), 0)
+    key_pos = lax.broadcasted_iota(jnp.int32, (positions, positions), 1)
+    lane = lax.broadcasted_iota(jnp.int32, (1, 2 * HEAD_DIM), 1)
+    first_lanes = lane < HEAD_DIM
+    keep = (first_lanes.astype(F32).astype(BF16), (lane >= HEAD_DIM).astype(F32).astype(BF16))
+
+    def row_sight():
+        same = (query_pos // ROWBLK) == (key_pos // ROWBLK)
+        return same, key_pos <= query_pos
+
+    def column_sight():
+        row, row2 = query_pos // cols, key_pos // cols
+        same = (row // COLBLK) == (row2 // COLBLK)
+        matching = lax.rem(query_pos, cols) == lax.rem(key_pos, cols)
+        return same, matching & (row2 <= row)
+
+    def softmax(head, query, key, sight):
+        bit = bits_ref[head : head + 1, :]
+        same, causal = sight
+        visible = causal & (same | (bit > 0))
+        scores = dot_nt(query, key) * (1.0 / math.sqrt(HEAD_DIM))
+        scores = jnp.where(visible, scores, -1e30)
+        weights = jnp.exp(scores - jnp.max(scores, axis=-1, keepdims=True))
+        return weights / jnp.sum(weights, axis=-1, keepdims=True)
+
+    def pair_of(pair):
+        return pl.ds(pair * 2 * HEAD_DIM, 2 * HEAD_DIM)
+
+    def merge(halves):
+        return jnp.where(first_lanes, halves[0], halves[1]).astype(BF16)
+
+    def forward(base, query, key, value, sight, slot):
+        outs = []
+        for side in range(2):
+            weights = softmax(base + side, query * keep[side], key, sight)
+            probs[slot + side] = weights
+            outs.append(dot_nn(weights.astype(BF16), value))
+        return merge(outs)
+
+    def backward(query, key, value, grad, slot):
+        grads = ([], [], [])
+        for side in range(2):
+            weights = probs[slot + side]
+            grad_side = grad * keep[side]
+            grad_probs = dot_nt(grad_side, value)
+            grad_scores = weights * (
+                grad_probs - jnp.sum(weights * grad_probs, axis=-1, keepdims=True)
+            )
+            grad_scores = (grad_scores * (1.0 / math.sqrt(HEAD_DIM))).astype(BF16)
+            grads[0].append(dot_nn(grad_scores, key))
+            grads[1].append(dot_tn(grad_scores, query))
+            grads[2].append(dot_tn(weights.astype(BF16), grad))
+        return [merge(grad_pair) for grad_pair in grads]
+
+    def rs_copy(which, hop):
+        if hop == 0:
+            src, dst, peer = part.at[which, :, :, 1 - core], part_recv1.at[which], core_peer
+        elif hop == 1:
+            src, dst, peer = acc1.at[which, other], part_recv2.at[which], x_peer
+        elif hop == 2:
+            src, dst, peer = acc2.at[which, :, 1 - y], part_recv3.at[which], y_peer
+        else:
+            z_there = lax.rem(z + hop - 2, z_count)
+            src, dst = acc3.at[which, z_there], part_recv4.at[which, hop - 3]
+            peer = (dp, z_there * 4 + y * 2 + core)
+        return pltpu.make_async_remote_copy(
+            src_ref=src,
+            dst_ref=dst,
+            send_sem=r_send_sem.at[which, hop],
+            recv_sem=r_recv_sem.at[which, hop],
+            device_id=peer,
+            device_id_type=MESH,
+        )
+
+    def rs_start(which, full):
+        part[which] = full.astype(BF16).reshape(part.shape[1:])
+        rs_copy(which, 0).start()
+
+    def rs_next(which, hop):
+        rs_copy(which, hop).wait_recv()
+        if hop == 0:
+            acc1[which] = (
+                part[which, :, :, core].astype(F32) + part_recv1[which].astype(F32)
+            ).astype(BF16)
+            rs_copy(which, 1).start()
+        elif hop == 1:
+            total = acc1[which, dp].astype(F32) + part_recv2[which].astype(F32)
+            acc2[which] = total.astype(BF16).reshape(acc2.shape[1:])
+            rs_copy(which, 2).start()
+        else:
+            acc3[which] = (
+                acc2[which, :, y].astype(F32) + part_recv3[which].astype(F32)
+            ).astype(BF16)
+            for step in range(1, z_count):
+                rs_copy(which, 2 + step).start()
+
+    def rs_end(which):
+        total = acc3[which, z].astype(F32)
+        for step in range(1, z_count):
+            rs_copy(which, 2 + step).wait_recv()
+            total = total + part_recv4[which, step - 1].astype(F32)
+        return total
+
+    share_weights(0)
+    for index in range(3):
+        qkv_send[index] = dot_nn(tokens_ref[...], w_full[index, :, split:]).astype(BF16)
+    exchange(qkv_send, qkv_recv, 0)
+
+    share_weights(1)
+    g_send[0] = dot_nt(cot_ref[...], wo_full[split:, :]).astype(BF16)
+    exchange(g_send, g_recv, 1)
+    g_rows[...] = dot_nt(cot_ref[...], wo_full[:split, :]).astype(BF16)
+
+    share_weights(2)
+    row_qkv = [dot_nn(tokens_ref[...], w_full[index, :, :split]).astype(BF16) for index in range(3)]
+    sight = row_sight()
+    for pair in range(split // (2 * HEAD_DIM)):
+        lanes = slice(pair * 2 * HEAD_DIM, (pair + 1) * 2 * HEAD_DIM)
+        query, key, value = (item[:, lanes] for item in row_qkv)
+        attended[:, pair_of(pair)] = forward(2 * pair, query, key, value, sight, 0)
+        grads = backward(query, key, value, g_rows[:, pair_of(pair)], 0)
+        for index in range(3):
+            row_grads[index, :, pair_of(pair)] = grads[index]
+
+    arrived(qkv_send, qkv_recv, 0)
+    half = split // HEAD_DIM
+    sight = column_sight()
+    for pair in range(split // (2 * HEAD_DIM)):
+        query, key, value = (qkv_recv[index, :, pair_of(pair)] for index in range(3))
+        out_send[0, :, pair_of(pair)] = forward(
+            half + 2 * pair, query, key, value, sight, 2 * pair
+        )
+    exchange(out_send, out_recv, 2)
+
+    arrived(g_send, g_recv, 1)
+    for pair in range(split // (2 * HEAD_DIM)):
+        query, key, value = (qkv_recv[index, :, pair_of(pair)] for index in range(3))
+        grads = backward(query, key, value, g_recv[0, :, pair_of(pair)], 2 * pair)
+        for index in range(3):
+            grad_send[index, :, pair_of(pair)] = grads[index]
+    exchange(grad_send, grad_recv, 3)
+
+    arrived(out_send, out_recv, 2)
+    attended[:, pl.ds(split, split)] = out_recv[0]
+    rs_start(0, dot_tn(cot_ref[...], attended[...]))
+    mixed_ref[...] = dot_nn(attended[...], wo_full[...]).astype(BF16)
+    rs_next(0, 0)
+    row_part = (
+        dot_nt(row_grads[0], w_full[0, :, :split])
+        + dot_nt(row_grads[1], w_full[1, :, :split])
+        + dot_nt(row_grads[2], w_full[2, :, :split])
+    )
+    part_value_rows = dot_tn(tokens_ref[...], row_grads[2])
+    rs_next(0, 1)
+
+    arrived(grad_send, grad_recv, 3)
+    part_value_cols = dot_tn(tokens_ref[...], grad_recv[2])
+    rs_start(1, jnp.concatenate([part_value_rows, part_value_cols], axis=1))
+    rs_next(0, 2)
+    rs_next(1, 0)
+    gtok_ref[...] = (
+        row_part
+        + dot_nt(grad_recv[0], w_full[0, :, split:])
+        + dot_nt(grad_recv[1], w_full[1, :, split:])
+        + dot_nt(grad_recv[2], w_full[2, :, split:])
+    ).astype(BF16)
+    gout_ref[...] = rs_end(0).T
+    rs_next(1, 1)
+    rs_next(1, 2)
+    gval_ref[...] = rs_end(1)
+
+    for group in range(3):
+        for hop in range(4):
+            weight_copy(group, hop).wait_send()
+    sent(qkv_send, qkv_recv, 0)
+    sent(g_send, g_recv, 1)
+    sent(out_send, out_recv, 2)
+    sent(grad_send, grad_recv, 3)
+    for which in range(2):
+        for hop in range(2 + z_count):
+            rs_copy(which, hop).wait_send()
+
+
+def fused_fits(dp_count, seq_count, tokens, row_mask, column_mask, w_query, w_out):
+    positions = tokens.shape[1] * tokens.shape[2]
+    return (
+        tokens.shape[0] == 1
+        and tokens.shape[1] == 1
+        and dp_count == 2
+        and seq_count % 4 == 0
+        and positions % (16 * seq_count) == 0
+        and w_query.shape[0] % 64 == 0
+        and w_out.shape[0] % 64 == 0
+        and tokens.shape[3] % (16 * dp_count * seq_count) == 0
+        and row_mask.shape[2] == 2
+        and column_mask.shape[2] == 2
+    )
+
+
+def fused_body(tokens, cotangent, row_mask, column_mask, w_query, w_key, w_value, w_out):
+    dp_count, seq_count = lax.axis_size("dp"), lax.axis_size("seq")
+    if not fused_fits(dp_count, seq_count, tokens, row_mask, column_mask, w_query, w_out):
+        return body(
+            tokens, cotangent, row_mask, column_mask, w_query, w_key, w_value, w_out
+        )
+    positions, width = tokens.shape[1] * tokens.shape[2], tokens.shape[3]
+    heads_width = w_query.shape[1]
+    split = heads_width // 2
+    rows = width // (dp_count * seq_count)
+    z_count = seq_count // 4
+    bits = jnp.concatenate(
+        [
+            jnp.broadcast_to(row_mask[:, 0, 1, 0][:, None], (row_mask.shape[0], positions)),
+            jnp.tile(column_mask[:, :, 1, 0], (1, seq_count)),
+        ],
+        axis=0,
+    ).astype(F32)
+    lead = (2, dp_count, seq_count // 2)
+    call = pl.pallas_call(
+        lambda *refs: fused_kernel(dp_count, seq_count, *refs),
+        out_shape=(
+            jax.ShapeDtypeStruct((positions, width), BF16),
+            jax.ShapeDtypeStruct((positions, width), BF16),
+            jax.ShapeDtypeStruct((rows, heads_width), F32),
+            jax.ShapeDtypeStruct((heads_width, rows), F32),
+        ),
+        in_specs=[pl.BlockSpec(memory_space=pltpu.VMEM)] * 7,
+        out_specs=[pl.BlockSpec(memory_space=pltpu.VMEM)] * 4,
+        scratch_shapes=[
+            pltpu.VMEM((3, width, heads_width), BF16),
+            pltpu.VMEM((heads_width, width), BF16),
+            pltpu.VMEM((3, positions, split), BF16),
+            pltpu.VMEM((3, positions, split), BF16),
+            pltpu.VMEM((positions, split), BF16),
+            pltpu.VMEM((1, positions, split), BF16),
+            pltpu.VMEM((1, positions, split), BF16),
+            pltpu.VMEM((1, positions, split), BF16),
+            pltpu.VMEM((1, positions, split), BF16),
+            pltpu.VMEM((3, positions, split), BF16),
+            pltpu.VMEM((3, positions, split), BF16),
+            pltpu.VMEM((3, positions, split), BF16),
+            pltpu.VMEM((split // HEAD_DIM, positions, positions), F32),
+            pltpu.VMEM((positions, heads_width), BF16),
+            pltpu.VMEM(lead + (2, rows, heads_width), BF16),
+            pltpu.VMEM(lead + (rows, heads_width), BF16),
+            pltpu.VMEM(lead + (rows, heads_width), BF16),
+            pltpu.VMEM((2, seq_count // 2, rows, heads_width), BF16),
+            pltpu.VMEM((2, z_count, 2, rows, heads_width), BF16),
+            pltpu.VMEM((2, z_count, rows, heads_width), BF16),
+            pltpu.VMEM((2, z_count, rows, heads_width), BF16),
+            pltpu.VMEM((2, z_count - 1, rows, heads_width), BF16),
+            pltpu.SemaphoreType.DMA((3, 4)),
+            pltpu.SemaphoreType.DMA((3, 4)),
+            pltpu.SemaphoreType.DMA((4, seq_count)),
+            pltpu.SemaphoreType.DMA((4, seq_count)),
+            pltpu.SemaphoreType.DMA((2, 2 + z_count)),
+            pltpu.SemaphoreType.DMA((2, 2 + z_count)),
+        ],
+        compiler_params=pltpu.CompilerParams(
+            collective_id=0, has_side_effects=True, vmem_limit_bytes=48 * 1024 * 1024
+        ),
+        cost_estimate=pl.CostEstimate(
+            flops=3_400_000_000, bytes_accessed=8_000_000, transcendentals=524288
+        ),
+    )
+    mixed, grad_tokens, grad_value, grad_output = call(
+        tokens.reshape(positions, width),
+        cotangent.reshape(positions, width),
+        bits,
+        w_query,
+        w_key,
+        w_value,
+        w_out,
+    )
+    return (
+        mixed.reshape(tokens.shape),
+        grad_tokens.reshape(tokens.shape),
+        grad_value,
+        grad_output,
+    )
+
+
 def solution(mesh):
     return jax.shard_map(
-        body,
+        fused_body,
         mesh=mesh,
         in_specs=(
             P("dp", "seq", None, None),

time: 334 us -> 91.9 us (0.28)
  waiting for transfers between devices: 212 us -> 0 us
  Pallas kernels: 0 us -> 80 us
  starting transfers between devices: 35 us -> 0 us
  local copies, waits for them, and re-layouts: 35.2 us -> 10.7 us
  matrix products: 23.9 us -> 0 us
  between operations: 14.6 us -> 0.65 us
  other arithmetic: 11.8 us -> 0.07 us
    unnamed x6 -> x0, waiting for transfers between devices: 107 us -> none
    pallas_call x0 -> x1, Pallas kernels: none -> 80 us  [fused_body(): call(tokens.reshape(positions, width), cotangent.reshape(positions, width...]
    all_gather x4 -> x0, waiting for transfers between devices: 74.9 us -> none  [the longest x1 22.4 us: body(): lax.all_gather(w_out, 'dp', axis=0, tiled=True)]
    all_to_all x8 -> x0, starting transfers between devices: 34.8 us -> none  [the longest x1 5.63 us: body(): lax.all_to_all(column_heads(value_flat), 'seq', split_axis=1, concat_axis...]
    all_to_all x8 -> x0, waiting for transfers between devices: 29.8 us -> none  [the longest x1 6.49 us: body(): lax.all_to_all(col_grads[1].reshape(grid_rows, cols_here, split), 'seq',...]
    dot_general x21 -> x0, matrix products: 23.3 us -> none  [the longest x5 6.55 us: attend(): jnp.einsum(forms[0], queries.astype(jnp.float32), key_part.astype(jnp.flo...]
    reshape x16 -> x0, local copies, waits for them, and re-layouts: 10.3 us -> none  [the longest x4 3.17 us: as_columns(): return block.reshape(grid_rows, cols_here, half, HEAD_DIM)]
    unnamed x78 -> x16, local copies, waits for them, and re-layouts: 15.5 us -> 9.2 us
  transfers between devices with their start and end apart: 13 -> 0, of which waited for: 12 -> 0; matrix products, arithmetic and copies ran while one was open for 14% -> 0% of each run, Pallas kernels for 0% -> 0%
where the time goes in v1:
time: 91.9 us; the launch traced here: 91.4 us
  Pallas kernels  80 us (87%)
  local copies, waits for them, and re-layouts  10.7 us (12%)
    pallas_call x1, Pallas kernels, fused_body(): call(tokens.reshape(positions, width), cotangent.reshape(positions, width...  80 us
    unnamed x16, local copies, waits for them, and re-layouts  9.2 us

profile of v1, /device:TPU:0, one launch (start us, length us, event | category | flops | bytes accessed | tf_op | source)
XLA Modules:
  0.0 91.4 jit_solution(9853730970683847438)
XLA Ops:
  0.6 0.7 slice_bitcast_fusion
  1.3 0.7 slice.7
  2.0 0.1 tile.12
  2.1 0.1 add_convert_fusion.refs_2_
  2.2 0.0 copy-start
  2.2 1.0 %copy-done = bf16[1,1,256,1024]{3,2,1,0:T(8,128)(2,1)S(1)} copy-done((bf16[1,1,256,1024]{3,2,1,0:T(8,128)(2,1)S(1)}, bf16[1,1,256,1024]{3,2,1,0:T(8,128)(2,1)}, u32[]{:S(2)}) %copy-start) | copy-done | bytes 524312
  3.2 0.0 copy-start.1
  3.2 1.0 %copy-done.1 = bf16[1,1,256,1024]{3,2,1,0:T(8,128)(2,1)S(1)} copy-done((bf16[1,1,256,1024]{3,2,1,0:T(8,128)(2,1)S(1)}, bf16[1,1,256,1024]{3,2,1,0:T(8,128)(2,1)}, u32[]{:S(2)}) %copy-start.1) | copy-done | bytes 524312
  4.3 0.0 copy-start.2
  4.3 1.0 %copy-done.2 = bf16[512,512]{1,0:T(8,128)(2,1)S(1)} copy-done((bf16[512,512]{1,0:T(8,128)(2,1)S(1)}, bf16[512,512]{1,0:T(8,128)(2,1)}, u32[]{:S(2)}) %copy-start.2) | copy-done | bytes 524312
  5.3 0.0 copy-start.3
  5.3 1.0 %copy-done.3 = bf16[512,512]{1,0:T(8,128)(2,1)S(1)} copy-done((bf16[512,512]{1,0:T(8,128)(2,1)S(1)}, bf16[512,512]{1,0:T(8,128)(2,1)}, u32[]{:S(2)}) %copy-start.3) | copy-done | bytes 524312
  6.3 0.0 copy-start.4
  6.3 1.0 %copy-done.4 = bf16[512,512]{1,0:T(8,128)(2,1)S(1)} copy-done((bf16[512,512]{1,0:T(8,128)(2,1)S(1)}, bf16[512,512]{1,0:T(8,128)(2,1)}, u32[]{:S(2)}) %copy-start.4) | copy-done | bytes 524312
  7.4 0.0 copy-start.5
  7.4 1.0 %copy-done.5 = bf16[256,1024]{1,0:T(8,128)(2,1)S(1)} copy-done((bf16[256,1024]{1,0:T(8,128)(2,1)S(1)}, bf16[256,1024]{1,0:T(8,128)(2,1)}, u32[]{:S(2)}) %copy-start.5) | copy-done | bytes 524312
  8.4 80.0 %shard_map.111 = (bf16[256,1024]{1,0:T(8,128)(2,1)S(1)}, bf16[256,1024]{1,0:T(8,128)(2,1)S(1)}, f32[32,512]{1,0:T(8,128)S(1)}, f32[512,32]{1,0:T(8,128)S(1)}) custom-call(bf16[256,1024]{1,0:T(8,128)(2,1)S(1)} %bitcast.9, bf16[256,1024]{1,0:T(8,128)(2,1)S(1)} %bitcast.10, f32[8,256]{1,0:T(8,128)S(1)} %add_convert_fusion.refs_2_, ...), custom_call_target="tpu_custom_call" | custom-call | flops 3400000000 | bytes 8000000 | tf_op jit(solution)/shard_map/pallas_call | solution.py:609
  88.5 0.7 copy.12
  89.2 0.8 copy.16
  90.0 0.8 copy.17
  90.8 0.6 copy.18
  (2 shorter events, 0.0 us)
Async XLA Ops:
  2.2 1.0 %copy-start = (bf16[1,1,256,1024]{3,2,1,0:T(8,128)(2,1)S(1)}, bf16[1,1,256,1024]{3,2,1,0:T(8,128)(2,1)}, u32[]{:S(2)}) copy-start(bf16[1,1,256,1024]{3,2,1,0:T(8,128)(2,1)} %param.8) | copy-start | bytes 1572868
  3.2 1.0 %copy-start.1 = (bf16[1,1,256,1024]{3,2,1,0:T(8,128)(2,1)S(1)}, bf16[1,1,256,1024]{3,2,1,0:T(8,128)(2,1)}, u32[]{:S(2)}) copy-start(bf16[1,1,256,1024]{3,2,1,0:T(8,128)(2,1)} %param.9) | copy-start | bytes 1572868
  4.3 1.0 %copy-start.2 = (bf16[512,512]{1,0:T(8,128)(2,1)S(1)}, bf16[512,512]{1,0:T(8,128)(2,1)}, u32[]{:S(2)}) copy-start(bf16[512,512]{1,0:T(8,128)(2,1)} %refs_3_.1) | copy-start | bytes 1572868
  5.3 1.0 %copy-start.3 = (bf16[512,512]{1,0:T(8,128)(2,1)S(1)}, bf16[512,512]{1,0:T(8,128)(2,1)}, u32[]{:S(2)}) copy-start(bf16[512,512]{1,0:T(8,128)(2,1)} %refs_4_.1) | copy-start | bytes 1572868
  6.3 1.0 %copy-start.4 = (bf16[512,512]{1,0:T(8,128)(2,1)S(1)}, bf16[512,512]{1,0:T(8,128)(2,1)}, u32[]{:S(2)}) copy-start(bf16[512,512]{1,0:T(8,128)(2,1)} %refs_5_.1) | copy-start | bytes 1572868
  7.4 1.0 %copy-start.5 = (bf16[256,1024]{1,0:T(8,128)(2,1)S(1)}, bf16[256,1024]{1,0:T(8,128)(2,1)}, u32[]{:S(2)}) copy-start(bf16[256,1024]{1,0:T(8,128)(2,1)} %refs_6_.1) | copy-start | bytes 1572868

commit v2 on v1

--- a/solution.py
+++ b/solution.py
@@ -193,17 +193,30 @@
 def fused_kernel(
     dp_count,
     seq_count,
+    tokens_hbm,
+    cot_hbm,
+    row_mask_hbm,
+    column_mask_hbm,
+    wq_hbm,
+    wk_hbm,
+    wv_hbm,
+    wo_hbm,
+    mixed_hbm,
+    gtok_hbm,
+    gval_hbm,
+    gout_hbm,
     tokens_ref,
     cot_ref,
-    bits_ref,
-    wq_ref,
-    wk_ref,
-    wv_ref,
-    wo_ref,
+    tokens_t,
+    cot_t,
+    row_mask_ref,
+    column_mask_ref,
+    bias,
     mixed_ref,
     gtok_ref,
     gval_ref,
     gout_ref,
+    gtok_part,
     w_full,
     wo_full,
     qkv_send,
@@ -232,6 +245,7 @@
     a_recv_sem,
     r_send_sem,
     r_recv_sem,
+    local_sem,
 ):
     dp = lax.axis_index("dp")
     seq = lax.axis_index("seq")
@@ -241,13 +255,37 @@
     z_count = seq_count // 4
     positions = tokens_ref.shape[0]
     cols = positions // seq_count
-    shard = wq_ref.shape[0]
-    out_shard = wo_ref.shape[0]
+    shard = wq_hbm.shape[0]
+    out_shard = wo_hbm.shape[0]
     split = qkv_send.shape[2]
+    half = split // HEAD_DIM
     other = 1 - dp
     x_peer = (other, seq)
     core_peer = (dp, seq + 1 - 2 * core)
     y_peer = (dp, seq + 2 - 4 * y)
+
+    own_rows = pl.ds(pl.multiple_of(dp * shard, shard), shard)
+    own_out = pl.ds(pl.multiple_of(dp * out_shard, out_shard), out_shard)
+    weights_in = [
+        pltpu.make_async_copy(wq_hbm, w_full.at[0, own_rows, :], local_sem.at[0]),
+        pltpu.make_async_copy(wk_hbm, w_full.at[1, own_rows, :], local_sem.at[1]),
+        pltpu.make_async_copy(wv_hbm, w_full.at[2, own_rows, :], local_sem.at[2]),
+        pltpu.make_async_copy(wo_hbm, wo_full.at[own_out, :], local_sem.at[3]),
+    ]
+    others_in = [
+        pltpu.make_async_copy(tokens_hbm, tokens_ref, local_sem.at[4]),
+        pltpu.make_async_copy(cot_hbm, cot_ref, local_sem.at[5]),
+        pltpu.make_async_copy(row_mask_hbm, row_mask_ref, local_sem.at[6]),
+        pltpu.make_async_copy(column_mask_hbm, column_mask_ref, local_sem.at[7]),
+    ]
+    outs = [
+        pltpu.make_async_copy(mixed_ref, mixed_hbm, local_sem.at[8]),
+        pltpu.make_async_copy(gtok_ref, gtok_hbm, local_sem.at[9]),
+        pltpu.make_async_copy(gval_ref, gval_hbm, local_sem.at[10]),
+        pltpu.make_async_copy(gout_ref, gout_hbm, local_sem.at[11]),
+    ]
+    for copy in weights_in + others_in:
+        copy.start()
 
     barrier = pltpu.get_barrier_semaphore()
     pl.semaphore_signal(barrier, inc=1, device_id=x_peer, device_id_type=MESH)
@@ -261,23 +299,20 @@
             device_id_type=MESH,
         )
 
-    own_rows = pl.ds(pl.multiple_of(dp * shard, shard), shard)
-    w_full[0, own_rows, :] = wq_ref[...]
-    w_full[1, own_rows, :] = wk_ref[...]
-    w_full[2, own_rows, :] = wv_ref[...]
-    own_out = pl.ds(pl.multiple_of(dp * out_shard, out_shard), out_shard)
-    wo_full[own_out, :] = wo_ref[...]
+    for copy in weights_in:
+        copy.wait()
     pl.semaphore_wait(barrier, seq_count)
 
     def region(group, owner, qy, qc):
-        if group == 1:
+        if group == 3:
             quarter = out_shard // 4
             start = pl.multiple_of(owner * out_shard + (qy * 2 + qc) * quarter, quarter)
             return wo_full.at[pl.ds(start, quarter), :]
         quarter = shard // 4
         start = pl.multiple_of(owner * shard + (qy * 2 + qc) * quarter, quarter)
-        lanes = pl.ds(split if group == 0 else 0, split)
-        return w_full.at[:, pl.ds(start, quarter), lanes]
+        if group == 4:
+            return w_full.at[:, pl.ds(start, quarter), pl.ds(0, split)]
+        return w_full.at[group, pl.ds(start, quarter), pl.ds(split, split)]
 
     def weight_copy(group, hop):
         if hop == 0:
@@ -297,14 +332,18 @@
             device_id_type=MESH,
         )
 
-    def share_weights(group):
+    def pass_on(group):
         weight_copy(group, 0).wait_recv()
-        if group < 2:
-            weight_copy(group + 1, 0).start()
+        if group + 2 < 5:
+            weight_copy(group + 2, 0).start()
         weight_copy(group, 1).start()
         weight_copy(group, 2).start()
+
+    def pass_core(group):
         weight_copy(group, 1).wait_recv()
         weight_copy(group, 3).start()
+
+    def weights_here(group):
         weight_copy(group, 2).wait_recv()
         weight_copy(group, 3).wait_recv()
 
@@ -321,6 +360,9 @@
             device_id_type=MESH,
         )
 
+    def one(ref, index):
+        return ref.at[pl.ds(index, 1)]
+
     def exchange(src, dst, phase):
         @pl.loop(1, seq_count)
         def _(step):
@@ -340,6 +382,7 @@
             column_copy(src, dst, phase, step).wait_send()
 
     weight_copy(0, 0).start()
+    weight_copy(1, 0).start()
 
     query_pos = lax.broadcasted_iota(jnp.int32, (positions, positions), 0)
     key_pos = lax.broadcasted_iota(jnp.int32, (positions, positions), 1)
@@ -347,24 +390,35 @@
     first_lanes = lane < HEAD_DIM
     keep = (first_lanes.astype(F32).astype(BF16), (lane >= HEAD_DIM).astype(F32).astype(BF16))
 
-    def row_sight():
-        same = (query_pos // ROWBLK) == (key_pos // ROWBLK)
-        return same, key_pos <= query_pos
-
-    def column_sight():
-        row, row2 = query_pos // cols, key_pos // cols
-        same = (row // COLBLK) == (row2 // COLBLK)
-        matching = lax.rem(query_pos, cols) == lax.rem(key_pos, cols)
-        return same, matching & (row2 <= row)
-
-    def softmax(head, query, key, sight):
-        bit = bits_ref[head : head + 1, :]
-        same, causal = sight
-        visible = causal & (same | (bit > 0))
-        scores = dot_nt(query, key) * (1.0 / math.sqrt(HEAD_DIM))
-        scores = jnp.where(visible, scores, -1e30)
+    def store_bias(index, seen):
+        bias[index] = jnp.where(seen, 0.0, -1e30)
+
+    row, row2 = query_pos // cols, key_pos // cols
+    matching = (lax.rem(query_pos, cols) == lax.rem(key_pos, cols)) & (row2 <= row)
+    store_bias(0, key_pos <= query_pos)
+    store_bias(1, (key_pos <= query_pos) & ((query_pos // ROWBLK) == (key_pos // ROWBLK)))
+    store_bias(2, matching)
+    store_bias(3, matching & ((row // COLBLK) == (row2 // COLBLK)))
+
+    for copy in others_in:
+        copy.wait()
+    tokens_t[...] = tokens_ref[...].T
+    cot_t[...] = cot_ref[...].T
+
+    def head_bias(head):
+        if head < half:
+            bit = row_mask_ref[head, 0, 1, 0]
+            return jnp.where(bit == 1, bias[0], bias[1])
+        column = lax.rem(lax.broadcasted_iota(jnp.int32, (1, positions), 1), cols)
+        bits = jnp.zeros((1, positions), jnp.int32)
+        for index in range(cols):
+            bits = jnp.where(column == index, column_mask_ref[head - half, index, 1, 0], bits)
+        return jnp.where(bits == 1, bias[2], bias[3])
+
+    def softmax(head, query, key):
+        scores = dot_nt(query, key) * (1.0 / math.sqrt(HEAD_DIM)) + head_bias(head)
         weights = jnp.exp(scores - jnp.max(scores, axis=-1, keepdims=True))
-        return weights / jnp.sum(weights, axis=-1, keepdims=True)
+        return weights * (1.0 / jnp.sum(weights, axis=-1, keepdims=True))
 
     def pair_of(pair):
         return pl.ds(pair * 2 * HEAD_DIM, 2 * HEAD_DIM)
@@ -372,10 +426,10 @@
     def merge(halves):
         return jnp.where(first_lanes, halves[0], halves[1]).astype(BF16)
 
-    def forward(base, query, key, value, sight, slot):
+    def forward(base, query, key, value, slot):
         outs = []
         for side in range(2):
-            weights = softmax(base + side, query * keep[side], key, sight)
+            weights = softmax(base + side, query * keep[side], key)
             probs[slot + side] = weights
             outs.append(dot_nn(weights.astype(BF16), value))
         return merge(outs)
@@ -444,84 +498,106 @@
             total = total + part_recv4[which, step - 1].astype(F32)
         return total
 
-    share_weights(0)
-    for index in range(3):
+    def project_columns(index):
+        weights_here(index)
         qkv_send[index] = dot_nn(tokens_ref[...], w_full[index, :, split:]).astype(BF16)
-    exchange(qkv_send, qkv_recv, 0)
-
-    share_weights(1)
+        exchange(one(qkv_send, index), one(qkv_recv, index), index)
+
+    for group in range(3):
+        pass_on(group)
+    for group in range(3):
+        pass_core(group)
+    project_columns(0)
+    project_columns(1)
+    pass_on(3)
+    project_columns(2)
+    pass_core(3)
+    pass_on(4)
+    weights_here(3)
     g_send[0] = dot_nt(cot_ref[...], wo_full[split:, :]).astype(BF16)
-    exchange(g_send, g_recv, 1)
+    exchange(g_send, g_recv, 3)
     g_rows[...] = dot_nt(cot_ref[...], wo_full[:split, :]).astype(BF16)
 
-    share_weights(2)
+    pass_core(4)
+    weights_here(4)
     row_qkv = [dot_nn(tokens_ref[...], w_full[index, :, :split]).astype(BF16) for index in range(3)]
-    sight = row_sight()
     for pair in range(split // (2 * HEAD_DIM)):
         lanes = slice(pair * 2 * HEAD_DIM, (pair + 1) * 2 * HEAD_DIM)
         query, key, value = (item[:, lanes] for item in row_qkv)
-        attended[:, pair_of(pair)] = forward(2 * pair, query, key, value, sight, 0)
+        attended[:, pair_of(pair)] = forward(2 * pair, query, key, value, 0)
         grads = backward(query, key, value, g_rows[:, pair_of(pair)], 0)
         for index in range(3):
             row_grads[index, :, pair_of(pair)] = grads[index]
-
-    arrived(qkv_send, qkv_recv, 0)
-    half = split // HEAD_DIM
-    sight = column_sight()
+    rs_start(0, dot_nn(cot_t[...], attended[:, :split]))
+    rs_start(1, dot_nn(tokens_t[...], row_grads[2]))
+
+    for index in range(3):
+        arrived(one(qkv_send, index), one(qkv_recv, index), index)
     for pair in range(split // (2 * HEAD_DIM)):
         query, key, value = (qkv_recv[index, :, pair_of(pair)] for index in range(3))
-        out_send[0, :, pair_of(pair)] = forward(
-            half + 2 * pair, query, key, value, sight, 2 * pair
-        )
-    exchange(out_send, out_recv, 2)
-
-    arrived(g_send, g_recv, 1)
+        out_send[0, :, pair_of(pair)] = forward(half + 2 * pair, query, key, value, 2 * pair)
+    exchange(out_send, out_recv, 4)
+    rs_next(0, 0)
+    rs_next(1, 0)
+
+    arrived(g_send, g_recv, 3)
     for pair in range(split // (2 * HEAD_DIM)):
         query, key, value = (qkv_recv[index, :, pair_of(pair)] for index in range(3))
         grads = backward(query, key, value, g_recv[0, :, pair_of(pair)], 2 * pair)
         for index in range(3):
             grad_send[index, :, pair_of(pair)] = grads[index]
-    exchange(grad_send, grad_recv, 3)
-
-    arrived(out_send, out_recv, 2)
+    exchange(grad_send, grad_recv, 5)
+    rs_next(0, 1)
+    rs_next(1, 1)
+
+    arrived(out_send, out_recv, 4)
     attended[:, pl.ds(split, split)] = out_recv[0]
-    rs_start(0, dot_tn(cot_ref[...], attended[...]))
+    rs_start(2, dot_nn(cot_t[...], out_recv[0]))
     mixed_ref[...] = dot_nn(attended[...], wo_full[...]).astype(BF16)
-    rs_next(0, 0)
-    row_part = (
+    outs[0].start()
+    rs_next(2, 0)
+    gtok_part[...] = (
         dot_nt(row_grads[0], w_full[0, :, :split])
         + dot_nt(row_grads[1], w_full[1, :, :split])
         + dot_nt(row_grads[2], w_full[2, :, :split])
     )
-    part_value_rows = dot_tn(tokens_ref[...], row_grads[2])
-    rs_next(0, 1)
-
-    arrived(grad_send, grad_recv, 3)
-    part_value_cols = dot_tn(tokens_ref[...], grad_recv[2])
-    rs_start(1, jnp.concatenate([part_value_rows, part_value_cols], axis=1))
     rs_next(0, 2)
-    rs_next(1, 0)
+    rs_next(1, 2)
+
+    arrived(grad_send, grad_recv, 5)
+    rs_start(3, dot_nn(tokens_t[...], grad_recv[2]))
+    rs_next(2, 1)
+    rs_next(3, 0)
     gtok_ref[...] = (
-        row_part
+        gtok_part[...]
         + dot_nt(grad_recv[0], w_full[0, :, split:])
         + dot_nt(grad_recv[1], w_full[1, :, split:])
         + dot_nt(grad_recv[2], w_full[2, :, split:])
     ).astype(BF16)
-    gout_ref[...] = rs_end(0).T
-    rs_next(1, 1)
-    rs_next(1, 2)
-    gval_ref[...] = rs_end(1)
-
-    for group in range(3):
+    outs[1].start()
+    rs_next(3, 1)
+    rs_next(2, 2)
+    gout_ref[:split, :] = rs_end(0).T
+    gval_ref[:, :split] = rs_end(1)
+    rs_next(3, 2)
+    gout_ref[split:, :] = rs_end(2).T
+    outs[3].start()
+    gval_ref[:, split:] = rs_end(3)
+    outs[2].start()
+
+    for group in range(5):
         for hop in range(4):
             weight_copy(group, hop).wait_send()
-    sent(qkv_send, qkv_recv, 0)
-    sent(g_send, g_recv, 1)
-    sent(out_send, out_recv, 2)
-    sent(grad_send, grad_recv, 3)
-    for which in range(2):
+    for index in range(3):
+        sent(one(qkv_send, index), one(qkv_recv, index), index)
+    sent(g_send, g_recv, 3)
+    sent(out_send, out_recv, 4)
+    sent(grad_send, grad_recv, 5)
+    for which in range(4):
         for hop in range(2 + z_count):
             rs_copy(which, hop).wait_send()
+    for copy in outs:
+        copy.wait()
 
 
 def fused_fits(dp_count, seq_count, tokens, row_mask, column_mask, w_query, w_out):
@@ -551,14 +627,7 @@
     split = heads_width // 2
     rows = width // (dp_count * seq_count)
     z_count = seq_count // 4
-    bits = jnp.concatenate(
-        [
-            jnp.broadcast_to(row_mask[:, 0, 1, 0][:, None], (row_mask.shape[0], positions)),
-            jnp.tile(column_mask[:, :, 1, 0], (1, seq_count)),
-        ],
-        axis=0,
-    ).astype(F32)
-    lead = (2, dp_count, seq_count // 2)
+    lead = (4, dp_count, seq_count // 2)
     call = pl.pallas_call(
         lambda *refs: fused_kernel(dp_count, seq_count, *refs),
         out_shape=(
@@ -567,9 +636,21 @@
             jax.ShapeDtypeStruct((rows, heads_width), F32),
             jax.ShapeDtypeStruct((heads_width, rows), F32),
         ),
-        in_specs=[pl.BlockSpec(memory_space=pltpu.VMEM)] * 7,
-        out_specs=[pl.BlockSpec(memory_space=pltpu.VMEM)] * 4,
+        in_specs=[pl.BlockSpec(memory_space=pl.ANY)] * 8,
+        out_specs=[pl.BlockSpec(memory_space=pl.ANY)] * 4,
         scratch_shapes=[
+            pltpu.VMEM((positions, width), BF16),
+            pltpu.VMEM((positions, width), BF16),
+            pltpu.VMEM((width, positions), BF16),
+            pltpu.VMEM((width, positions), BF16),
+            pltpu.SMEM(row_mask.shape, jnp.int32),
+            pltpu.SMEM(column_mask.shape, jnp.int32),
+            pltpu.VMEM((4, positions, positions), F32),
+            pltpu.VMEM((positions, width), BF16),
+            pltpu.VMEM((positions, width), BF16),
+            pltpu.VMEM((rows, heads_width), F32),
+            pltpu.VMEM((heads_width, rows), F32),
+            pltpu.VMEM((positions, width), F32),
             pltpu.VMEM((3, width, heads_width), BF16),
             pltpu.VMEM((heads_width, width), BF16),
             pltpu.VMEM((3, positions, split), BF16),
@@ -584,20 +665,21 @@
             pltpu.VMEM((3, positions, split), BF16),
             pltpu.VMEM((split // HEAD_DIM, positions, positions), F32),
             pltpu.VMEM((positions, heads_width), BF16),
-            pltpu.VMEM(lead + (2, rows, heads_width), BF16),
-            pltpu.VMEM(lead + (rows, heads_width), BF16),
-            pltpu.VMEM(lead + (rows, heads_width), BF16),
-            pltpu.VMEM((2, seq_count // 2, rows, heads_width), BF16),
-            pltpu.VMEM((2, z_count, 2, rows, heads_width), BF16),
-            pltpu.VMEM((2, z_count, rows, heads_width), BF16),
-            pltpu.VMEM((2, z_count, rows, heads_width), BF16),
-            pltpu.VMEM((2, z_count - 1, rows, heads_width), BF16),
-            pltpu.SemaphoreType.DMA((3, 4)),
-            pltpu.SemaphoreType.DMA((3, 4)),
-            pltpu.SemaphoreType.DMA((4, seq_count)),
-            pltpu.SemaphoreType.DMA((4, seq_count)),
-            pltpu.SemaphoreType.DMA((2, 2 + z_count)),
-            pltpu.SemaphoreType.DMA((2, 2 + z_count)),
+            pltpu.VMEM(lead + (2, rows, split), BF16),
+            pltpu.VMEM(lead + (rows, split), BF16),
+            pltpu.VMEM(lead + (rows, split), BF16),
+            pltpu.VMEM((4, seq_count // 2, rows, split), BF16),
+            pltpu.VMEM((4, z_count, 2, rows, split), BF16),
+            pltpu.VMEM((4, z_count, rows, split), BF16),
+            pltpu.VMEM((4, z_count, rows, split), BF16),
+            pltpu.VMEM((4, z_count - 1, rows, split), BF16),
+            pltpu.SemaphoreType.DMA((5, 4)),
+            pltpu.SemaphoreType.DMA((5, 4)),
+            pltpu.SemaphoreType.DMA((6, seq_count)),
+            pltpu.SemaphoreType.DMA((6, seq_count)),
+            pltpu.SemaphoreType.DMA((4, 2 + z_count)),
+            pltpu.SemaphoreType.DMA((4, 2 + z_count)),
+            pltpu.SemaphoreType.DMA((12,)),
         ],
         compiler_params=pltpu.CompilerParams(
             collective_id=0, has_side_effects=True, vmem_limit_bytes=48 * 1024 * 1024
@@ -609,7 +691,8 @@
     mixed, grad_tokens, grad_value, grad_output = call(
         tokens.reshape(positions, width),
         cotangent.reshape(positions, width),
-        bits,
+        row_mask,
+        column_mask,
         w_query,
         w_key,
         w_value,

time: 91.9 us -> 78.6 us (0.86)
  Pallas kernels: 80 us -> 67.4 us
    pallas_call x1, Pallas kernels: 80 us -> 67.4 us  [fused_body(): call(tokens.reshape(positions, width), cotangent.reshape(positions, width...]
    unnamed x16 -> x20, local copies, waits for them, and re-layouts: 9.2 us -> 10.1 us
where the time goes in v2:
time: 78.6 us; the launch traced here: 78.2 us
  Pallas kernels  67.4 us (86%)
  local copies, waits for them, and re-layouts  10.1 us (13%)
    pallas_call x1, Pallas kernels, fused_body(): call(tokens.reshape(positions, width), cotangent.reshape(positions, width...  67.4 us
    unnamed x20, local copies, waits for them, and re-layouts  10.1 us

profile of v2, /device:TPU:0, one launch (start us, length us, event | category | flops | bytes accessed | tf_op | source)
XLA Modules:
  0.0 78.2 jit_solution(16329431190839543320)
XLA Ops:
  0.6 0.0 copy-start.6
  0.6 0.8 copy.12.refs_2_
  1.4 0.0 copy-done.6
  1.4 0.1 copy.13.refs_3_
  1.6 0.0 copy-start
  1.6 1.0 %copy-done = bf16[1,1,256,1024]{3,2,1,0:T(8,128)(2,1)S(1)} copy-done((bf16[1,1,256,1024]{3,2,1,0:T(8,128)(2,1)S(1)}, bf16[1,1,256,1024]{3,2,1,0:T(8,128)(2,1)}, u32[]{:S(2)}) %copy-start) | copy-done | bytes 524312
  2.6 0.0 copy-start.1
  2.6 1.0 %copy-done.1 = bf16[1,1,256,1024]{3,2,1,0:T(8,128)(2,1)S(1)} copy-done((bf16[1,1,256,1024]{3,2,1,0:T(8,128)(2,1)S(1)}, bf16[1,1,256,1024]{3,2,1,0:T(8,128)(2,1)}, u32[]{:S(2)}) %copy-start.1) | copy-done | bytes 524312
  3.6 0.0 copy-start.2
  3.6 1.0 %copy-done.2 = bf16[512,512]{1,0:T(8,128)(2,1)S(1)} copy-done((bf16[512,512]{1,0:T(8,128)(2,1)S(1)}, bf16[512,512]{1,0:T(8,128)(2,1)}, u32[]{:S(2)}) %copy-start.2) | copy-done | bytes 524312
  4.7 0.0 copy-start.3
  4.7 1.0 %copy-done.3 = bf16[512,512]{1,0:T(8,128)(2,1)S(1)} copy-done((bf16[512,512]{1,0:T(8,128)(2,1)S(1)}, bf16[512,512]{1,0:T(8,128)(2,1)}, u32[]{:S(2)}) %copy-start.3) | copy-done | bytes 524312
  5.7 0.0 copy-start.4
  5.7 1.0 %copy-done.4 = bf16[512,512]{1,0:T(8,128)(2,1)S(1)} copy-done((bf16[512,512]{1,0:T(8,128)(2,1)S(1)}, bf16[512,512]{1,0:T(8,128)(2,1)}, u32[]{:S(2)}) %copy-start.4) | copy-done | bytes 524312
  6.8 0.0 copy-start.5
  6.8 1.0 %copy-done.5 = bf16[256,1024]{1,0:T(8,128)(2,1)S(1)} copy-done((bf16[256,1024]{1,0:T(8,128)(2,1)S(1)}, bf16[256,1024]{1,0:T(8,128)(2,1)}, u32[]{:S(2)}) %copy-start.5) | copy-done | bytes 524312
  7.8 67.4 %shard_map.111 = (bf16[256,1024]{1,0:T(8,128)(2,1)S(1)}, bf16[256,1024]{1,0:T(8,128)(2,1)S(1)}, f32[32,512]{1,0:T(8,128)S(1)}, f32[512,32]{1,0:T(8,128)S(1)}) custom-call(bf16[256,1024]{1,0:T(8,128)(2,1)S(1)} %bitcast.6, bf16[256,1024]{1,0:T(8,128)(2,1)S(1)} %bitcast.7, s32[4,1,2,2]{3,2,1,0:T(2,128)S(1)} %copy.12.refs_2_, s32[4,16,2,2]{3,2,1,0:T(2,128)S(1)} %copy.13.refs_3_, ...), custom_call_target="tpu_custom_call" | custom-call | flops 3400000000 | bytes 8000000 | tf_op jit(solution)/shard_map/pallas_call | solution.py:691
  75.2 0.7 copy.14
  76.0 0.8 %copy.18 = bf16[1,1,256,1024]{3,2,1,0:T(8,128)(2,1)} copy(bf16[1,1,256,1024]{3,2,1,0:T(8,128)(2,1)S(1)} %bitcast.5) | data formatting | bytes 1048576
  76.8 0.8 %copy.19 = bf16[1,1,256,1024]{3,2,1,0:T(8,128)(2,1)} copy(bf16[1,1,256,1024]{3,2,1,0:T(8,128)(2,1)S(1)} %bitcast.4) | data formatting | bytes 1048576
  77.6 0.6 copy.20
Async XLA Ops:
  0.6 0.8 %copy-start.6 = (s32[4,16,2,2]{1,3,2,0:T(2,128)S(1)}, s32[4,16,2,2]{1,3,2,0:T(2,128)}, u32[]{:S(2)}) copy-start(s32[4,16,2,2]{1,3,2,0:T(2,128)} %param.11) | copy-start | bytes 3076
  1.6 1.0 %copy-start = (bf16[1,1,256,1024]{3,2,1,0:T(8,128)(2,1)S(1)}, bf16[1,1,256,1024]{3,2,1,0:T(8,128)(2,1)}, u32[]{:S(2)}) copy-start(bf16[1,1,256,1024]{3,2,1,0:T(8,128)(2,1)} %param.8) | copy-start | bytes 1572868
  2.6 1.0 %copy-start.1 = (bf16[1,1,256,1024]{3,2,1,0:T(8,128)(2,1)S(1)}, bf16[1,1,256,1024]{3,2,1,0:T(8,128)(2,1)}, u32[]{:S(2)}) copy-start(bf16[1,1,256,1024]{3,2,1,0:T(8,128)(2,1)} %param.9) | copy-start | bytes 1572868
  3.6 1.0 %copy-start.2 = (bf16[512,512]{1,0:T(8,128)(2,1)S(1)}, bf16[512,512]{1,0:T(8,128)(2,1)}, u32[]{:S(2)}) copy-start(bf16[512,512]{1,0:T(8,128)(2,1)} %refs_4_.1) | copy-start | bytes 1572868
  4.7 1.0 %copy-start.3 = (bf16[512,512]{1,0:T(8,128)(2,1)S(1)}, bf16[512,512]{1,0:T(8,128)(2,1)}, u32[]{:S(2)}) copy-start(bf16[512,512]{1,0:T(8,128)(2,1)} %refs_5_.1) | copy-start | bytes 1572868
  5.7 1.0 %copy-start.4 = (bf16[512,512]{1,0:T(8,128)(2,1)S(1)}, bf16[512,512]{1,0:T(8,128)(2,1)}, u32[]{:S(2)}) copy-start(bf16[512,512]{1,0:T(8,128)(2,1)} %refs_6_.1) | copy-start | bytes 1572868
  6.8 1.0 %copy-start.5 = (bf16[256,1024]{1,0:T(8,128)(2,1)S(1)}, bf16[256,1024]{1,0:T(8,128)(2,1)}, u32[]{:S(2)}) copy-start(bf16[256,1024]{1,0:T(8,128)(2,1)} %refs_7_.1) | copy-start | bytes 1572868

commit v3 on v2

--- a/solution.py
+++ b/solution.py
@@ -290,7 +290,7 @@
     barrier = pltpu.get_barrier_semaphore()
     pl.semaphore_signal(barrier, inc=1, device_id=x_peer, device_id_type=MESH)
 
-    @pl.loop(1, seq_count)
+    @pl.loop(1, seq_count, unroll=True)
     def _(step):
         pl.semaphore_signal(
             barrier,
@@ -354,8 +354,8 @@
         return pltpu.make_async_remote_copy(
             src_ref=src.at[:, there, :],
             dst_ref=dst.at[:, here, :],
-            send_sem=a_send_sem.at[phase, step],
-            recv_sem=a_recv_sem.at[phase, step],
+            send_sem=a_send_sem.at[phase],
+            recv_sem=a_recv_sem.at[phase],
             device_id=(dp, target),
             device_id_type=MESH,
         )
@@ -364,22 +364,29 @@
         return ref.at[pl.ds(index, 1)]
 
     def exchange(src, dst, phase):
-        @pl.loop(1, seq_count)
+        @pl.loop(1, seq_count, unroll=True)
         def _(step):
             column_copy(src, dst, phase, step).start()
 
         here = pl.ds(pl.multiple_of(seq * cols, cols), cols)
         dst[:, here, :] = src[:, here, :]
 
+    def whole_exchange(src, dst, phase):
+        many = pl.ds(0, positions - cols)
+        return pltpu.make_async_remote_copy(
+            src_ref=src.at[:, many, :],
+            dst_ref=dst.at[:, many, :],
+            send_sem=a_send_sem.at[phase],
+            recv_sem=a_recv_sem.at[phase],
+            device_id=core_peer,
+            device_id_type=MESH,
+        )
+
     def arrived(src, dst, phase):
-        @pl.loop(1, seq_count)
-        def _(step):
-            column_copy(src, dst, phase, step).wait_recv()
+        whole_exchange(src, dst, phase).wait_recv()
 
     def sent(src, dst, phase):
-        @pl.loop(1, seq_count)
-        def _(step):
-            column_copy(src, dst, phase, step).wait_send()
+        whole_exchange(src, dst, phase).wait_send()
 
     weight_copy(0, 0).start()
     weight_copy(1, 0).start()
@@ -402,17 +409,15 @@
 
     for copy in others_in:
         copy.wait()
-    tokens_t[...] = tokens_ref[...].T
-    cot_t[...] = cot_ref[...].T
 
     def head_bias(head):
         if head < half:
-            bit = row_mask_ref[head, 0, 1, 0]
+            bit = row_mask_ref[0, 1, 0, head]
             return jnp.where(bit == 1, bias[0], bias[1])
         column = lax.rem(lax.broadcasted_iota(jnp.int32, (1, positions), 1), cols)
         bits = jnp.zeros((1, positions), jnp.int32)
         for index in range(cols):
-            bits = jnp.where(column == index, column_mask_ref[head - half, index, 1, 0], bits)
+            bits = jnp.where(column == index, column_mask_ref[head - half, 1, 0, index], bits)
         return jnp.where(bits == 1, bias[2], bias[3])
 
     def softmax(head, query, key):
@@ -503,12 +508,14 @@
         qkv_send[index] = dot_nn(tokens_ref[...], w_full[index, :, split:]).astype(BF16)
         exchange(one(qkv_send, index), one(qkv_recv, index), index)
 
-    for group in range(3):
-        pass_on(group)
-    for group in range(3):
-        pass_core(group)
+    pass_on(0)
+    pass_on(1)
+    pass_core(0)
+    pass_on(2)
     project_columns(0)
+    pass_core(1)
     project_columns(1)
+    pass_core(2)
     pass_on(3)
     project_columns(2)
     pass_core(3)
@@ -517,8 +524,25 @@
     g_send[0] = dot_nt(cot_ref[...], wo_full[split:, :]).astype(BF16)
     exchange(g_send, g_recv, 3)
     g_rows[...] = dot_nt(cot_ref[...], wo_full[:split, :]).astype(BF16)
-
+    tokens_t[...] = tokens_ref[...].T
+    cot_t[...] = cot_ref[...].T
+
+    for index in range(3):
+        arrived(one(qkv_send, index), one(qkv_recv, index), index)
+    for pair in range(split // (2 * HEAD_DIM)):
+        query, key, value = (qkv_recv[index, :, pair_of(pair)] for index in range(3))
+        out_send[0, :, pair_of(pair)] = forward(half + 2 * pair, query, key, value, 2 * pair)
+    exchange(out_send, out_recv, 4)
     pass_core(4)
+
+    arrived(g_send, g_recv, 3)
+    for pair in range(split // (2 * HEAD_DIM)):
+        query, key, value = (qkv_recv[index, :, pair_of(pair)] for index in range(3))
+        grads = backward(query, key, value, g_recv[0, :, pair_of(pair)], 2 * pair)
+        for index in range(3):
+            grad_send[index, :, pair_of(pair)] = grads[index]
+    exchange(grad_send, grad_recv, 5)
+
     weights_here(4)
     row_qkv = [dot_nn(tokens_ref[...], w_full[index, :, :split]).astype(BF16) for index in range(3)]
     for pair in range(split // (2 * HEAD_DIM)):
@@ -531,43 +555,25 @@
     rs_start(0, dot_nn(cot_t[...], attended[:, :split]))
     rs_start(1, dot_nn(tokens_t[...], row_grads[2]))
 
-    for index in range(3):
-        arrived(one(qkv_send, index), one(qkv_recv, index), index)
-    for pair in range(split // (2 * HEAD_DIM)):
-        query, key, value = (qkv_recv[index, :, pair_of(pair)] for index in range(3))
-        out_send[0, :, pair_of(pair)] = forward(half + 2 * pair, query, key, value, 2 * pair)
-    exchange(out_send, out_recv, 4)
+    arrived(out_send, out_recv, 4)
+    rs_start(2, dot_nn(cot_t[...], out_recv[0]))
     rs_next(0, 0)
     rs_next(1, 0)
-
-    arrived(g_send, g_recv, 3)
-    for pair in range(split // (2 * HEAD_DIM)):
-        query, key, value = (qkv_recv[index, :, pair_of(pair)] for index in range(3))
-        grads = backward(query, key, value, g_recv[0, :, pair_of(pair)], 2 * pair)
-        for index in range(3):
-            grad_send[index, :, pair_of(pair)] = grads[index]
-    exchange(grad_send, grad_recv, 5)
-    rs_next(0, 1)
-    rs_next(1, 1)
-
-    arrived(out_send, out_recv, 4)
     attended[:, pl.ds(split, split)] = out_recv[0]
-    rs_start(2, dot_nn(cot_t[...], out_recv[0]))
     mixed_ref[...] = dot_nn(attended[...], wo_full[...]).astype(BF16)
     outs[0].start()
     rs_next(2, 0)
+
+    arrived(grad_send, grad_recv, 5)
+    rs_start(3, dot_nn(tokens_t[...], grad_recv[2]))
+    rs_next(0, 1)
     gtok_part[...] = (
         dot_nt(row_grads[0], w_full[0, :, :split])
         + dot_nt(row_grads[1], w_full[1, :, :split])
         + dot_nt(row_grads[2], w_full[2, :, :split])
     )
-    rs_next(0, 2)
-    rs_next(1, 2)
-
-    arrived(grad_send, grad_recv, 5)
-    rs_start(3, dot_nn(tokens_t[...], grad_recv[2]))
-    rs_next(2, 1)
     rs_next(3, 0)
+    rs_next(1, 1)
     gtok_ref[...] = (
         gtok_part[...]
         + dot_nt(grad_recv[0], w_full[0, :, split:])
@@ -575,16 +581,9 @@
         + dot_nt(grad_recv[2], w_full[2, :, split:])
     ).astype(BF16)
     outs[1].start()
-    rs_next(3, 1)
-    rs_next(2, 2)
-    gout_ref[:split, :] = rs_end(0).T
-    gval_ref[:, :split] = rs_end(1)
-    rs_next(3, 2)
-    gout_ref[split:, :] = rs_end(2).T
-    outs[3].start()
-    gval_ref[:, split:] = rs_end(3)
-    outs[2].start()
-
+    rs_next(2, 1)
+    rs_next(0, 2)
+    rs_next(1, 2)
     for group in range(5):
         for hop in range(4):
             weight_copy(group, hop).wait_send()
@@ -593,11 +592,46 @@
     sent(g_send, g_recv, 3)
     sent(out_send, out_recv, 4)
     sent(grad_send, grad_recv, 5)
-    for which in range(4):
+    rs_next(3, 1)
+    rs_next(2, 2)
+    gout_ref[:, :split] = rs_end(0)
+    gval_ref[:, :split] = rs_end(1)
+    rs_next(3, 2)
+    gout_ref[:, split:] = rs_end(2)
+    outs[3].start()
+    for which in range(3):
         for hop in range(2 + z_count):
             rs_copy(which, hop).wait_send()
+    gval_ref[:, split:] = rs_end(3)
+    outs[2].start()
+    for hop in range(2 + z_count):
+        rs_copy(3, hop).wait_send()
     for copy in outs:
         copy.wait()
+
+
+def hand_out_kernel(*refs):
+    count = len(refs) // 2
+    sems = refs[-1]
+    copies = [
+        pltpu.make_async_copy(refs[index], refs[count + index], sems.at[index])
+        for index in range(count)
+    ]
+    for copy in copies:
+        copy.start()
+    for copy in copies:
+        copy.wait()
+
+
+def hand_out(*arrays):
+    return pl.pallas_call(
+        hand_out_kernel,
+        out_shape=[jax.ShapeDtypeStruct(item.shape, item.dtype) for item in arrays],
+        in_specs=[pl.BlockSpec(memory_space=pltpu.HBM)] * len(arrays),
+        out_specs=[pl.BlockSpec(memory_space=pltpu.HBM)] * len(arrays),
+        scratch_shapes=[pltpu.SemaphoreType.DMA((len(arrays),))],
+        compiler_params=pltpu.CompilerParams(vmem_limit_bytes=64 * 1024 * 1024 - 65536),
+    )(*arrays)
 
 
 def fused_fits(dp_count, seq_count, tokens, row_mask, column_mask, w_query, w_out):
@@ -627,6 +661,8 @@
     split = heads_width // 2
     rows = width // (dp_count * seq_count)
     z_count = seq_count // 4
+    stored_row_mask = jnp.transpose(row_mask, (1, 2, 3, 0))
+    stored_column_mask = jnp.transpose(column_mask, (0, 2, 3, 1))
     lead = (4, dp_count, seq_count // 2)
     call = pl.pallas_call(
         lambda *refs: fused_kernel(dp_count, seq_count, *refs),
@@ -634,22 +670,22 @@
             jax.ShapeDtypeStruct((positions, width), BF16),
             jax.ShapeDtypeStruct((positions, width), BF16),
             jax.ShapeDtypeStruct((rows, heads_width), F32),
-            jax.ShapeDtypeStruct((heads_width, rows), F32),
-        ),
-        in_specs=[pl.BlockSpec(memory_space=pl.ANY)] * 8,
-        out_specs=[pl.BlockSpec(memory_space=pl.ANY)] * 4,
+            jax.ShapeDtypeStruct((rows, heads_width), F32),
+        ),
+        in_specs=[pl.BlockSpec(memory_space=pltpu.HBM)] * 8,
+        out_specs=[pl.BlockSpec(memory_space=pltpu.HBM)] * 4,
         scratch_shapes=[
             pltpu.VMEM((positions, width), BF16),
             pltpu.VMEM((positions, width), BF16),
             pltpu.VMEM((width, positions), BF16),
             pltpu.VMEM((width, positions), BF16),
-            pltpu.SMEM(row_mask.shape, jnp.int32),
-            pltpu.SMEM(column_mask.shape, jnp.int32),
+            pltpu.SMEM(stored_row_mask.shape, jnp.int32),
+            pltpu.SMEM(stored_column_mask.shape, jnp.int32),
             pltpu.VMEM((4, positions, positions), F32),
             pltpu.VMEM((positions, width), BF16),
             pltpu.VMEM((positions, width), BF16),
             pltpu.VMEM((rows, heads_width), F32),
-            pltpu.VMEM((heads_width, rows), F32),
+            pltpu.VMEM((rows, heads_width), F32),
             pltpu.VMEM((positions, width), F32),
             pltpu.VMEM((3, width, heads_width), BF16),
             pltpu.VMEM((heads_width, width), BF16),
@@ -675,14 +711,14 @@
             pltpu.VMEM((4, z_count - 1, rows, split), BF16),
             pltpu.SemaphoreType.DMA((5, 4)),
             pltpu.SemaphoreType.DMA((5, 4)),
-            pltpu.SemaphoreType.DMA((6, seq_count)),
-            pltpu.SemaphoreType.DMA((6, seq_count)),
+            pltpu.SemaphoreType.DMA((6,)),
+            pltpu.SemaphoreType.DMA((6,)),
             pltpu.SemaphoreType.DMA((4, 2 + z_count)),
             pltpu.SemaphoreType.DMA((4, 2 + z_count)),
             pltpu.SemaphoreType.DMA((12,)),
         ],
         compiler_params=pltpu.CompilerParams(
-            collective_id=0, has_side_effects=True, vmem_limit_bytes=48 * 1024 * 1024
+            collective_id=0, has_side_effects=True, vmem_limit_bytes=64 * 1024 * 1024 - 65536
         ),
         cost_estimate=pl.CostEstimate(
             flops=3_400_000_000, bytes_accessed=8_000_000, transcendentals=524288
@@ -691,18 +727,21 @@
     mixed, grad_tokens, grad_value, grad_output = call(
         tokens.reshape(positions, width),
         cotangent.reshape(positions, width),
-        row_mask,
-        column_mask,
+        stored_row_mask,
+        stored_column_mask,
         w_query,
         w_key,
         w_value,
         w_out,
     )
+    mixed, grad_tokens, grad_value, grad_output = hand_out(
+        mixed, grad_tokens, grad_value, grad_output
+    )
     return (
         mixed.reshape(tokens.shape),
         grad_tokens.reshape(tokens.shape),
         grad_value,
-        grad_output,
+        jnp.transpose(grad_output),
     )
 
 

time: 78.6 us -> 97.2 us (1.24)
  Pallas kernels: 67.4 us -> 96.4 us
  local copies, waits for them, and re-layouts: 10.1 us -> 0 us
    pallas_call x0 -> x1, Pallas kernels: none -> 36.9 us  [hand_out(): pl.pallas_call(hand_out_kernel, out_shape=[jax.ShapeDtypeStruct(item.shap...]
    unnamed x20 -> x0, local copies, waits for them, and re-layouts: 10.1 us -> none
    pallas_call x1, Pallas kernels: 67.4 us -> 59.6 us  [fused_body(): call(tokens.reshape(positions, width), cotangent.reshape(positions, width...]
where the time goes in v3:
time: 97.2 us; the launch traced here: 97.1 us
  Pallas kernels  96.4 us (99%)
    pallas_call x1, Pallas kernels, fused_body(): call(tokens.reshape(positions, width), cotangent.reshape(positions, width...  59.6 us
    pallas_call x1, Pallas kernels, hand_out(): pl.pallas_call(hand_out_kernel, out_shape=[jax.ShapeDtypeStruct(item.shap...  36.9 us

profile of v3, /device:TPU:0, one launch (start us, length us, event | category | flops | bytes accessed | tf_op | source)
XLA Modules:
  0.0 97.1 jit_solution(8784240286588141123)
XLA Ops:
  0.6 59.6 %shard_map.111 = (bf16[256,1024]{1,0:T(8,128)(2,1)}, bf16[256,1024]{1,0:T(8,128)(2,1)}, f32[32,512]{1,0:T(8,128)}, f32[32,512]{1,0:T(8,128)}) custom-call(bf16[256,1024]{1,0:T(8,128)(2,1)} %bitcast.7, bf16[256,1024]{1,0:T(8,128)(2,1)} %bitcast.8, s32[1,2,2,4]{3,2,1,0:T(2,128)} %bitcast.13, s32[4,2,2,16]{3,2,1,0:T(2,128)} %bitcast.12, ...), custom_call_target="tpu_custom_call" | custom-call | flops 3400000000 | bytes 8000000 | tf_op jit(solution)/shard_map/pallas_call | solution.py:727
  60.2 36.9 %shard_map.112 = (bf16[256,1024]{1,0:T(8,128)(2,1)}, bf16[256,1024]{1,0:T(8,128)(2,1)}, f32[32,512]{1,0:T(8,128)}, f32[32,512]{1,0:T(8,128)}) custom-call(bf16[256,1024]{1,0:T(8,128)(2,1)} %get-tuple-element.12.refs_0_, bf16[256,1024]{1,0:T(8,128)(2,1)} %get-tuple-element.13.refs_1_, f32[32,512]{1,0:T(8,128)} %get-tuple-element.14.refs_2_, ...), custom_call_target="tpu_custom_call" | custom-call | tf_op jit(solution)/shard_map/pallas_call | solution.py:627

commit v4 on v3

--- a/solution.py
+++ b/solution.py
@@ -228,14 +228,17 @@
     out_recv,
     grad_send,
     grad_recv,
+    row_qkv,
     row_grads,
     probs,
     attended,
     part,
     part_recv1,
     acc1,
-    part_recv2,
-    acc2,
+    recv_x_first,
+    recv_y_first,
+    acc_x_first,
+    acc_y_first,
     part_recv3,
     acc3,
     part_recv4,
@@ -439,28 +442,35 @@
             outs.append(dot_nn(weights.astype(BF16), value))
         return merge(outs)
 
-    def backward(query, key, value, grad, slot):
-        grads = ([], [], [])
+    def value_grad(grad, slot):
+        sides = [dot_tn(probs[slot + side].astype(BF16), grad) for side in range(2)]
+        return merge(sides)
+
+    def query_key_grads(query, key, value, grad, slot):
+        grads = ([], [])
         for side in range(2):
             weights = probs[slot + side]
-            grad_side = grad * keep[side]
-            grad_probs = dot_nt(grad_side, value)
+            grad_probs = dot_nt(grad * keep[side], value)
             grad_scores = weights * (
                 grad_probs - jnp.sum(weights * grad_probs, axis=-1, keepdims=True)
             )
             grad_scores = (grad_scores * (1.0 / math.sqrt(HEAD_DIM))).astype(BF16)
             grads[0].append(dot_nn(grad_scores, key))
             grads[1].append(dot_tn(grad_scores, query))
-            grads[2].append(dot_tn(weights.astype(BF16), grad))
         return [merge(grad_pair) for grad_pair in grads]
 
     def rs_copy(which, hop):
+        piece, order = which // 2, which % 2
         if hop == 0:
-            src, dst, peer = part.at[which, :, :, 1 - core], part_recv1.at[which], core_peer
+            src, dst, peer = part.at[which, :, :, :, 1 - core], part_recv1.at[which], core_peer
+        elif hop == 1 and order == 0:
+            src, dst, peer = acc1.at[which, other], recv_x_first.at[piece], x_peer
         elif hop == 1:
-            src, dst, peer = acc1.at[which, other], part_recv2.at[which], x_peer
+            src, dst, peer = acc1.at[which, :, :, 1 - y], recv_y_first.at[piece], y_peer
+        elif hop == 2 and order == 0:
+            src, dst, peer = acc_x_first.at[piece, :, 1 - y], part_recv3.at[which], y_peer
         elif hop == 2:
-            src, dst, peer = acc2.at[which, :, 1 - y], part_recv3.at[which], y_peer
+            src, dst, peer = acc_y_first.at[piece, other], part_recv3.at[which], x_peer
         else:
             z_there = lax.rem(z + hop - 2, z_count)
             src, dst = acc3.at[which, z_there], part_recv4.at[which, hop - 3]
@@ -474,34 +484,51 @@
             device_id_type=MESH,
         )
 
-    def rs_start(which, full):
-        part[which] = full.astype(BF16).reshape(part.shape[1:])
-        rs_copy(which, 0).start()
-
-    def rs_next(which, hop):
-        rs_copy(which, hop).wait_recv()
-        if hop == 0:
-            acc1[which] = (
-                part[which, :, :, core].astype(F32) + part_recv1[which].astype(F32)
-            ).astype(BF16)
-            rs_copy(which, 1).start()
-        elif hop == 1:
-            total = acc1[which, dp].astype(F32) + part_recv2[which].astype(F32)
-            acc2[which] = total.astype(BF16).reshape(acc2.shape[1:])
-            rs_copy(which, 2).start()
-        else:
-            acc3[which] = (
-                acc2[which, :, y].astype(F32) + part_recv3[which].astype(F32)
-            ).astype(BF16)
+    def rs_start(piece, full):
+        lanes = split // 2
+        for order in range(2):
+            half_piece = full[:, order * lanes : (order + 1) * lanes].astype(BF16)
+            part[2 * piece + order] = half_piece.reshape(part.shape[1:])
+            rs_copy(2 * piece + order, 0).start()
+
+    def rs_next(piece, hop):
+        for order in range(2):
+            which = 2 * piece + order
+            rs_copy(which, hop).wait_recv()
+            if hop == 0:
+                acc1[which] = (
+                    part[which, :, :, :, core].astype(F32) + part_recv1[which].astype(F32)
+                ).astype(BF16)
+            elif hop == 1 and order == 0:
+                acc_x_first[piece] = (
+                    acc1[which, dp].astype(F32) + recv_x_first[piece].astype(F32)
+                ).astype(BF16)
+            elif hop == 1:
+                acc_y_first[piece] = (
+                    acc1[which, :, :, y].astype(F32) + recv_y_first[piece].astype(F32)
+                ).astype(BF16)
+            elif order == 0:
+                acc3[which] = (
+                    acc_x_first[piece, :, y].astype(F32) + part_recv3[which].astype(F32)
+                ).astype(BF16)
+            else:
+                acc3[which] = (
+                    acc_y_first[piece, dp].astype(F32) + part_recv3[which].astype(F32)
+                ).astype(BF16)
+            if hop < 2:
+                rs_copy(which, hop + 1).start()
+            else:
+                for step in range(1, z_count):
+                    rs_copy(which, 2 + step).start()
+
+    def rs_end(piece, out, first_lane):
+        for order in range(2):
+            which = 2 * piece + order
+            total = acc3[which, z].astype(F32)
             for step in range(1, z_count):
-                rs_copy(which, 2 + step).start()
-
-    def rs_end(which):
-        total = acc3[which, z].astype(F32)
-        for step in range(1, z_count):
-            rs_copy(which, 2 + step).wait_recv()
-            total = total + part_recv4[which, step - 1].astype(F32)
-        return total
+                rs_copy(which, 2 + step).wait_recv()
+                total = total + part_recv4[which, step - 1].astype(F32)
+            out[:, pl.ds(first_lane + order * (split // 2), split // 2)] = total
 
     def project_columns(index):
         weights_here(index)
@@ -536,44 +563,60 @@
     pass_core(4)
 
     arrived(g_send, g_recv, 3)
-    for pair in range(split // (2 * HEAD_DIM)):
+    pairs = range(split // (2 * HEAD_DIM))
+    for pair in pairs:
+        grad_send[2, :, pair_of(pair)] = value_grad(g_recv[0, :, pair_of(pair)], 2 * pair)
+    exchange(one(grad_send, 2), one(grad_recv, 2), 5)
+    for pair in pairs:
         query, key, value = (qkv_recv[index, :, pair_of(pair)] for index in range(3))
-        grads = backward(query, key, value, g_recv[0, :, pair_of(pair)], 2 * pair)
-        for index in range(3):
+        grads = query_key_grads(query, key, value, g_recv[0, :, pair_of(pair)], 2 * pair)
+        for index in range(2):
             grad_send[index, :, pair_of(pair)] = grads[index]
-    exchange(grad_send, grad_recv, 5)
+    exchange(grad_send.at[pl.ds(0, 2)], grad_recv.at[pl.ds(0, 2)], 6)
 
     weights_here(4)
-    row_qkv = [dot_nn(tokens_ref[...], w_full[index, :, :split]).astype(BF16) for index in range(3)]
-    for pair in range(split // (2 * HEAD_DIM)):
-        lanes = slice(pair * 2 * HEAD_DIM, (pair + 1) * 2 * HEAD_DIM)
-        query, key, value = (item[:, lanes] for item in row_qkv)
-        attended[:, pair_of(pair)] = forward(2 * pair, query, key, value, 0)
-        grads = backward(query, key, value, g_rows[:, pair_of(pair)], 0)
-        for index in range(3):
-            row_grads[index, :, pair_of(pair)] = grads[index]
+    for index in range(3):
+        row_qkv[index] = dot_nn(tokens_ref[...], w_full[index, :, :split]).astype(BF16)
+    for pair in pairs:
+        query, key, value = (row_qkv[index, :, pair_of(pair)] for index in range(3))
+        slot = half + 2 * pair
+        attended[:, pair_of(pair)] = forward(2 * pair, query, key, value, slot)
+        row_grads[2, :, pair_of(pair)] = value_grad(g_rows[:, pair_of(pair)], slot)
     rs_start(0, dot_nn(cot_t[...], attended[:, :split]))
     rs_start(1, dot_nn(tokens_t[...], row_grads[2]))
-
     arrived(out_send, out_recv, 4)
     rs_start(2, dot_nn(cot_t[...], out_recv[0]))
     rs_next(0, 0)
+    arrived(one(grad_send, 2), one(grad_recv, 2), 5)
+    rs_start(3, dot_nn(tokens_t[...], grad_recv[2]))
     rs_next(1, 0)
+
+    def row_query_key(pair):
+        query, key, value = (row_qkv[index, :, pair_of(pair)] for index in range(3))
+        grads = query_key_grads(query, key, value, g_rows[:, pair_of(pair)], half + 2 * pair)
+        for index in range(2):
+            row_grads[index, :, pair_of(pair)] = grads[index]
+
+    for pair in pairs:
+        row_query_key(pair)
+        if pair == 0:
+            rs_next(2, 0)
+            rs_next(3, 0)
+    rs_next(0, 1)
+    rs_next(1, 1)
     attended[:, pl.ds(split, split)] = out_recv[0]
     mixed_ref[...] = dot_nn(attended[...], wo_full[...]).astype(BF16)
     outs[0].start()
-    rs_next(2, 0)
-
-    arrived(grad_send, grad_recv, 5)
-    rs_start(3, dot_nn(tokens_t[...], grad_recv[2]))
-    rs_next(0, 1)
+    rs_next(2, 1)
     gtok_part[...] = (
         dot_nt(row_grads[0], w_full[0, :, :split])
         + dot_nt(row_grads[1], w_full[1, :, :split])
         + dot_nt(row_grads[2], w_full[2, :, :split])
     )
-    rs_next(3, 0)
-    rs_next(1, 1)
+    rs_next(3, 1)
+    rs_next(0, 2)
+    rs_next(1, 2)
+    arrived(grad_send.at[pl.ds(0, 2)], grad_recv.at[pl.ds(0, 2)], 6)
     gtok_ref[...] = (
         gtok_part[...]
         + dot_nt(grad_recv[0], w_full[0, :, split:])
@@ -581,9 +624,8 @@
         + dot_nt(grad_recv[2], w_full[2, :, split:])
     ).astype(BF16)
     outs[1].start()
-    rs_next(2, 1)
-    rs_next(0, 2)
-    rs_next(1, 2)
+    rs_next(2, 2)
+    rs_next(3, 2)
     for group in range(5):
         for hop in range(4):
             weight_copy(group, hop).wait_send()
@@ -591,45 +633,50 @@
         sent(one(qkv_send, index), one(qkv_recv, index), index)
     sent(g_send, g_recv, 3)
     sent(out_send, out_recv, 4)
-    sent(grad_send, grad_recv, 5)
-    rs_next(3, 1)
-    rs_next(2, 2)
-    gout_ref[:, :split] = rs_end(0)
-    gval_ref[:, :split] = rs_end(1)
-    rs_next(3, 2)
-    gout_ref[:, split:] = rs_end(2)
+    sent(one(grad_send, 2), one(grad_recv, 2), 5)
+    sent(grad_send.at[pl.ds(0, 2)], grad_recv.at[pl.ds(0, 2)], 6)
+    rs_end(0, gout_ref, 0)
+    rs_end(2, gout_ref, split)
     outs[3].start()
-    for which in range(3):
+    rs_end(1, gval_ref, 0)
+    rs_end(3, gval_ref, split)
+    outs[2].start()
+    for which in range(8):
         for hop in range(2 + z_count):
             rs_copy(which, hop).wait_send()
-    gval_ref[:, split:] = rs_end(3)
-    outs[2].start()
-    for hop in range(2 + z_count):
-        rs_copy(3, hop).wait_send()
     for copy in outs:
         copy.wait()
 
 
 def hand_out_kernel(*refs):
-    count = len(refs) // 2
-    sems = refs[-1]
-    copies = [
-        pltpu.make_async_copy(refs[index], refs[count + index], sems.at[index])
+    count = (len(refs) - 2) // 3
+    ins, outs, held = refs[:count], refs[count : 2 * count], refs[2 * count : 3 * count]
+    in_sems, out_sems = refs[-2:]
+    fetches = [
+        pltpu.make_async_copy(ins[index], held[index], in_sems.at[index]) for index in range(count)
+    ]
+    stores = [
+        pltpu.make_async_copy(held[index], outs[index], out_sems.at[index])
         for index in range(count)
     ]
-    for copy in copies:
+    for copy in fetches:
         copy.start()
-    for copy in copies:
+    for index in range(count):
+        fetches[index].wait()
+        stores[index].start()
+    for copy in stores:
         copy.wait()
 
 
 def hand_out(*arrays):
+    count = len(arrays)
     return pl.pallas_call(
         hand_out_kernel,
         out_shape=[jax.ShapeDtypeStruct(item.shape, item.dtype) for item in arrays],
-        in_specs=[pl.BlockSpec(memory_space=pltpu.HBM)] * len(arrays),
-        out_specs=[pl.BlockSpec(memory_space=pltpu.HBM)] * len(arrays),
-        scratch_shapes=[pltpu.SemaphoreType.DMA((len(arrays),))],
+        in_specs=[pl.BlockSpec(memory_space=pltpu.HBM)] * count,
+        out_specs=[pl.BlockSpec(memory_space=pltpu.HBM)] * count,
+        scratch_shapes=[pltpu.VMEM(item.shape, item.dtype) for item in arrays]
+        + [pltpu.SemaphoreType.DMA((count,)), pltpu.SemaphoreType.DMA((count,))],
         compiler_params=pltpu.CompilerParams(vmem_limit_bytes=64 * 1024 * 1024 - 65536),
     )(*arrays)
 
@@ -643,6 +690,7 @@
         and seq_count % 4 == 0
         and positions % (16 * seq_count) == 0
         and w_query.shape[0] % 64 == 0
+        and w_query.shape[1] % 512 == 0
         and w_out.shape[0] % 64 == 0
         and tokens.shape[3] % (16 * dp_count * seq_count) == 0
         and row_mask.shape[2] == 2
@@ -663,7 +711,8 @@
     z_count = seq_count // 4
     stored_row_mask = jnp.transpose(row_mask, (1, 2, 3, 0))
     stored_column_mask = jnp.transpose(column_mask, (0, 2, 3, 1))
-    lead = (4, dp_count, seq_count // 2)
+    lead = (8, dp_count, z_count, 2)
+    lanes = split // 2
     call = pl.pallas_call(
         lambda *refs: fused_kernel(dp_count, seq_count, *refs),
         out_shape=(
@@ -699,22 +748,25 @@
             pltpu.VMEM((3, positions, split), BF16),
             pltpu.VMEM((3, positions, split), BF16),
             pltpu.VMEM((3, positions, split), BF16),
-            pltpu.VMEM((split // HEAD_DIM, positions, positions), F32),
+            pltpu.VMEM((3, positions, split), BF16),
+            pltpu.VMEM((heads_width // HEAD_DIM, positions, positions), F32),
             pltpu.VMEM((positions, heads_width), BF16),
-            pltpu.VMEM(lead + (2, rows, split), BF16),
-            pltpu.VMEM(lead + (rows, split), BF16),
-            pltpu.VMEM(lead + (rows, split), BF16),
-            pltpu.VMEM((4, seq_count // 2, rows, split), BF16),
-            pltpu.VMEM((4, z_count, 2, rows, split), BF16),
-            pltpu.VMEM((4, z_count, rows, split), BF16),
-            pltpu.VMEM((4, z_count, rows, split), BF16),
-            pltpu.VMEM((4, z_count - 1, rows, split), BF16),
+            pltpu.VMEM(lead + (2, rows, lanes), BF16),
+            pltpu.VMEM(lead + (rows, lanes), BF16),
+            pltpu.VMEM(lead + (rows, lanes), BF16),
+            pltpu.VMEM((4, z_count, 2, rows, lanes), BF16),
+            pltpu.VMEM((4, 2, z_count, rows, lanes), BF16),
+            pltpu.VMEM((4, z_count, 2, rows, lanes), BF16),
+            pltpu.VMEM((4, 2, z_count, rows, lanes), BF16),
+            pltpu.VMEM((8, z_count, rows, lanes), BF16),
+            pltpu.VMEM((8, z_count, rows, lanes), BF16),
+            pltpu.VMEM((8, z_count - 1, rows, lanes), BF16),
             pltpu.SemaphoreType.DMA((5, 4)),
             pltpu.SemaphoreType.DMA((5, 4)),
-            pltpu.SemaphoreType.DMA((6,)),
-            pltpu.SemaphoreType.DMA((6,)),
-            pltpu.SemaphoreType.DMA((4, 2 + z_count)),
-            pltpu.SemaphoreType.DMA((4, 2 + z_count)),
+            pltpu.SemaphoreType.DMA((7,)),
+            pltpu.SemaphoreType.DMA((7,)),
+            pltpu.SemaphoreType.DMA((8, 2 + z_count)),
+            pltpu.SemaphoreType.DMA((8, 2 + z_count)),
             pltpu.SemaphoreType.DMA((12,)),
         ],
         compiler_params=pltpu.CompilerParams(

time: 97.2 us -> 59.3 us (0.61)
  Pallas kernels: 96.4 us -> 58.6 us
    pallas_call x1, Pallas kernels: 36.9 us -> 2.11 us  [hand_out(): pl.pallas_call(hand_out_kernel, out_shape=[jax.ShapeDtypeStruct(item.shap...]
    pallas_call x1, Pallas kernels: 59.6 us -> 56.4 us  [fused_body(): call(tokens.reshape(positions, width), cotangent.reshape(positions, width...]
where the time goes in v4:
time: 59.3 us; the launch traced here: 59.2 us
  Pallas kernels  58.6 us (99%)
  between operations  0.64 us (1%)
    pallas_call x1, Pallas kernels, fused_body(): call(tokens.reshape(positions, width), cotangent.reshape(positions, width...  56.4 us
    pallas_call x1, Pallas kernels, hand_out(): pl.pallas_call(hand_out_kernel, out_shape=[jax.ShapeDtypeStruct(item.shap...  2.11 us

profile of v4, /device:TPU:0, one launch (start us, length us, event | category | flops | bytes accessed | tf_op | source)
XLA Modules:
  0.0 59.2 jit_solution(17595581779902458511)
XLA Ops:
  0.6 56.4 %shard_map.111 = (bf16[256,1024]{1,0:T(8,128)(2,1)}, bf16[256,1024]{1,0:T(8,128)(2,1)}, f32[32,512]{1,0:T(8,128)}, f32[32,512]{1,0:T(8,128)}) custom-call(bf16[256,1024]{1,0:T(8,128)(2,1)} %bitcast.7, bf16[256,1024]{1,0:T(8,128)(2,1)} %bitcast.8, s32[1,2,2,4]{3,2,1,0:T(2,128)} %bitcast.13, s32[4,2,2,16]{3,2,1,0:T(2,128)} %bitcast.12, ...), custom_call_target="tpu_custom_call" | custom-call | flops 3400000000 | bytes 8000000 | tf_op jit(solution)/shard_map/pallas_call | solution.py:779
  57.1 2.1 %shard_map.112 = (bf16[256,1024]{1,0:T(8,128)(2,1)}, bf16[256,1024]{1,0:T(8,128)(2,1)}, f32[32,512]{1,0:T(8,128)}, f32[32,512]{1,0:T(8,128)}) custom-call(bf16[256,1024]{1,0:T(8,128)(2,1)} %get-tuple-element.12.refs_0_, bf16[256,1024]{1,0:T(8,128)(2,1)} %get-tuple-element.13.refs_1_, f32[32,512]{1,0:T(8,128)} %get-tuple-element.14.refs_2_, ...), custom_call_target="tpu_custom_call" | custom-call | tf_op jit(solution)/shard_map/pallas_call | solution.py:673

commit v5 on v4

--- a/solution.py
+++ b/solution.py
@@ -307,13 +307,13 @@
     pl.semaphore_wait(barrier, seq_count)
 
     def region(group, owner, qy, qc):
-        if group == 3:
+        if group == 4:
             quarter = out_shard // 4
             start = pl.multiple_of(owner * out_shard + (qy * 2 + qc) * quarter, quarter)
             return wo_full.at[pl.ds(start, quarter), :]
         quarter = shard // 4
         start = pl.multiple_of(owner * shard + (qy * 2 + qc) * quarter, quarter)
-        if group == 4:
+        if group == 3:
             return w_full.at[:, pl.ds(start, quarter), pl.ds(0, split)]
         return w_full.at[group, pl.ds(start, quarter), pl.ds(split, split)]
 
@@ -535,6 +535,12 @@
         qkv_send[index] = dot_nn(tokens_ref[...], w_full[index, :, split:]).astype(BF16)
         exchange(one(qkv_send, index), one(qkv_recv, index), index)
 
+    pairs = range(split // (2 * HEAD_DIM))
+
+    def row_forward(pair):
+        query, key, value = (row_qkv[index, :, pair_of(pair)] for index in range(3))
+        attended[:, pair_of(pair)] = forward(2 * pair, query, key, value, half + 2 * pair)
+
     pass_on(0)
     pass_on(1)
     pass_core(0)
@@ -545,25 +551,30 @@
     pass_core(2)
     pass_on(3)
     project_columns(2)
+    tokens_t[...] = tokens_ref[...].T
     pass_core(3)
     pass_on(4)
+    cot_t[...] = cot_ref[...].T
     weights_here(3)
+    for index in range(3):
+        row_qkv[index] = dot_nn(tokens_ref[...], w_full[index, :, :split]).astype(BF16)
+    pass_core(4)
+    row_forward(0)
+    weights_here(4)
     g_send[0] = dot_nt(cot_ref[...], wo_full[split:, :]).astype(BF16)
     exchange(g_send, g_recv, 3)
     g_rows[...] = dot_nt(cot_ref[...], wo_full[:split, :]).astype(BF16)
-    tokens_t[...] = tokens_ref[...].T
-    cot_t[...] = cot_ref[...].T
+    for pair in pairs[1:]:
+        row_forward(pair)
 
     for index in range(3):
         arrived(one(qkv_send, index), one(qkv_recv, index), index)
-    for pair in range(split // (2 * HEAD_DIM)):
+    for pair in pairs:
         query, key, value = (qkv_recv[index, :, pair_of(pair)] for index in range(3))
         out_send[0, :, pair_of(pair)] = forward(half + 2 * pair, query, key, value, 2 * pair)
     exchange(out_send, out_recv, 4)
-    pass_core(4)
 
     arrived(g_send, g_recv, 3)
-    pairs = range(split // (2 * HEAD_DIM))
     for pair in pairs:
         grad_send[2, :, pair_of(pair)] = value_grad(g_recv[0, :, pair_of(pair)], 2 * pair)
     exchange(one(grad_send, 2), one(grad_recv, 2), 5)
@@ -574,22 +585,16 @@
             grad_send[index, :, pair_of(pair)] = grads[index]
     exchange(grad_send.at[pl.ds(0, 2)], grad_recv.at[pl.ds(0, 2)], 6)
 
-    weights_here(4)
-    for index in range(3):
-        row_qkv[index] = dot_nn(tokens_ref[...], w_full[index, :, :split]).astype(BF16)
     for pair in pairs:
-        query, key, value = (row_qkv[index, :, pair_of(pair)] for index in range(3))
-        slot = half + 2 * pair
-        attended[:, pair_of(pair)] = forward(2 * pair, query, key, value, slot)
-        row_grads[2, :, pair_of(pair)] = value_grad(g_rows[:, pair_of(pair)], slot)
+        row_grads[2, :, pair_of(pair)] = value_grad(g_rows[:, pair_of(pair)], half + 2 * pair)
+    rs_start(1, dot_nn(tokens_t[...], row_grads[2]))
     rs_start(0, dot_nn(cot_t[...], attended[:, :split]))
-    rs_start(1, dot_nn(tokens_t[...], row_grads[2]))
     arrived(out_send, out_recv, 4)
     rs_start(2, dot_nn(cot_t[...], out_recv[0]))
-    rs_next(0, 0)
+    rs_next(1, 0)
     arrived(one(grad_send, 2), one(grad_recv, 2), 5)
     rs_start(3, dot_nn(tokens_t[...], grad_recv[2]))
-    rs_next(1, 0)
+    rs_next(0, 0)
 
     def row_query_key(pair):
         query, key, value = (row_qkv[index, :, pair_of(pair)] for index in range(3))

time: 59.3 us -> 64.3 us (1.084)
  Pallas kernels: 58.6 us -> 63.5 us
    pallas_call x1, Pallas kernels: 56.4 us -> 61.4 us  [fused_body(): call(tokens.reshape(positions, width), cotangent.reshape(positions, width...]
where the time goes in v5:
time: 64.3 us; the launch traced here: 64.1 us
  Pallas kernels  63.5 us (99%)
    pallas_call x1, Pallas kernels, fused_body(): call(tokens.reshape(positions, width), cotangent.reshape(positions, width...  61.4 us
    pallas_call x1, Pallas kernels, hand_out(): pl.pallas_call(hand_out_kernel, out_shape=[jax.ShapeDtypeStruct(item.shap...  2.11 us

profile of v5, /device:TPU:0, one launch (start us, length us, event | category | flops | bytes accessed | tf_op | source)
XLA Modules:
  0.0 64.1 jit_solution(1094663065797483632)
XLA Ops:
  0.6 61.4 %shard_map.111 = (bf16[256,1024]{1,0:T(8,128)(2,1)}, bf16[256,1024]{1,0:T(8,128)(2,1)}, f32[32,512]{1,0:T(8,128)}, f32[32,512]{1,0:T(8,128)}) custom-call(bf16[256,1024]{1,0:T(8,128)(2,1)} %bitcast.7, bf16[256,1024]{1,0:T(8,128)(2,1)} %bitcast.8, s32[1,2,2,4]{3,2,1,0:T(2,128)} %bitcast.13, s32[4,2,2,16]{3,2,1,0:T(2,128)} %bitcast.12, ...), custom_call_target="tpu_custom_call" | custom-call | flops 3400000000 | bytes 8000000 | tf_op jit(solution)/shard_map/pallas_call | solution.py:784
  62.0 2.1 %shard_map.112 = (bf16[256,1024]{1,0:T(8,128)(2,1)}, bf16[256,1024]{1,0:T(8,128)(2,1)}, f32[32,512]{1,0:T(8,128)}, f32[32,512]{1,0:T(8,128)}) custom-call(bf16[256,1024]{1,0:T(8,128)(2,1)} %get-tuple-element.12.refs_0_, bf16[256,1024]{1,0:T(8,128)(2,1)} %get-tuple-element.13.refs_1_, f32[32,512]{1,0:T(8,128)} %get-tuple-element.14.refs_2_, ...), custom_call_target="tpu_custom_call" | custom-call | tf_op jit(solution)/shard_map/pallas_call | solution.py:678

commit v6 on v4

--- a/solution.py
+++ b/solution.py
@@ -307,13 +307,14 @@
     pl.semaphore_wait(barrier, seq_count)
 
     def region(group, owner, qy, qc):
-        if group == 3:
+        if group in (3, 4):
             quarter = out_shard // 4
             start = pl.multiple_of(owner * out_shard + (qy * 2 + qc) * quarter, quarter)
-            return wo_full.at[pl.ds(start, quarter), :]
+            width = wo_full.shape[1] // 2
+            return wo_full.at[pl.ds(start, quarter), pl.ds((group - 3) * width, width)]
         quarter = shard // 4
         start = pl.multiple_of(owner * shard + (qy * 2 + qc) * quarter, quarter)
-        if group == 4:
+        if group == 5:
             return w_full.at[:, pl.ds(start, quarter), pl.ds(0, split)]
         return w_full.at[group, pl.ds(start, quarter), pl.ds(split, split)]
 
@@ -337,8 +338,10 @@
 
     def pass_on(group):
         weight_copy(group, 0).wait_recv()
-        if group + 2 < 5:
+        if group < 3:
             weight_copy(group + 2, 0).start()
+        elif group == 4:
+            weight_copy(5, 0).start()
         weight_copy(group, 1).start()
         weight_copy(group, 2).start()
 
@@ -394,8 +397,6 @@
     weight_copy(0, 0).start()
     weight_copy(1, 0).start()
 
-    query_pos = lax.broadcasted_iota(jnp.int32, (positions, positions), 0)
-    key_pos = lax.broadcasted_iota(jnp.int32, (positions, positions), 1)
     lane = lax.broadcasted_iota(jnp.int32, (1, 2 * HEAD_DIM), 1)
     first_lanes = lane < HEAD_DIM
     keep = (first_lanes.astype(F32).astype(BF16), (lane >= HEAD_DIM).astype(F32).astype(BF16))
@@ -403,12 +404,16 @@
     def store_bias(index, seen):
         bias[index] = jnp.where(seen, 0.0, -1e30)
 
-    row, row2 = query_pos // cols, key_pos // cols
-    matching = (lax.rem(query_pos, cols) == lax.rem(key_pos, cols)) & (row2 <= row)
-    store_bias(0, key_pos <= query_pos)
-    store_bias(1, (key_pos <= query_pos) & ((query_pos // ROWBLK) == (key_pos // ROWBLK)))
-    store_bias(2, matching)
-    store_bias(3, matching & ((row // COLBLK) == (row2 // COLBLK)))
+    def build_bias():
+        query_pos = lax.broadcasted_iota(jnp.int32, (positions, positions), 0)
+        key_pos = lax.broadcasted_iota(jnp.int32, (positions, positions), 1)
+        differ = query_pos ^ key_pos
+        causal = key_pos <= query_pos
+        matching = causal & ((differ & (cols - 1)) == 0)
+        store_bias(0, causal)
+        store_bias(1, causal & (differ < ROWBLK))
+        store_bias(2, matching)
+        store_bias(3, matching & (differ < COLBLK * cols))
 
     for copy in others_in:
         copy.wait()
@@ -541,18 +546,22 @@
     pass_on(2)
     project_columns(0)
     pass_core(1)
+    pass_on(3)
     project_columns(1)
     pass_core(2)
-    pass_on(3)
+    pass_on(4)
     project_columns(2)
     pass_core(3)
-    pass_on(4)
+    pass_core(4)
     weights_here(3)
+    weights_here(4)
     g_send[0] = dot_nt(cot_ref[...], wo_full[split:, :]).astype(BF16)
     exchange(g_send, g_recv, 3)
+    build_bias()
     g_rows[...] = dot_nt(cot_ref[...], wo_full[:split, :]).astype(BF16)
     tokens_t[...] = tokens_ref[...].T
     cot_t[...] = cot_ref[...].T
+    pass_on(5)
 
     for index in range(3):
         arrived(one(qkv_send, index), one(qkv_recv, index), index)
@@ -560,7 +569,7 @@
         query, key, value = (qkv_recv[index, :, pair_of(pair)] for index in range(3))
         out_send[0, :, pair_of(pair)] = forward(half + 2 * pair, query, key, value, 2 * pair)
     exchange(out_send, out_recv, 4)
-    pass_core(4)
+    pass_core(5)
 
     arrived(g_send, g_recv, 3)
     pairs = range(split // (2 * HEAD_DIM))
@@ -574,7 +583,7 @@
             grad_send[index, :, pair_of(pair)] = grads[index]
     exchange(grad_send.at[pl.ds(0, 2)], grad_recv.at[pl.ds(0, 2)], 6)
 
-    weights_here(4)
+    weights_here(5)
     for index in range(3):
         row_qkv[index] = dot_nn(tokens_ref[...], w_full[index, :, :split]).astype(BF16)
     for pair in pairs:
@@ -626,7 +635,7 @@
     outs[1].start()
     rs_next(2, 2)
     rs_next(3, 2)
-    for group in range(5):
+    for group in range(6):
         for hop in range(4):
             weight_copy(group, hop).wait_send()
     for index in range(3):
@@ -691,6 +700,9 @@
         and positions % (16 * seq_count) == 0
         and w_query.shape[0] % 64 == 0
         and w_query.shape[1] % 512 == 0
+        and w_out.shape[1] % 256 == 0
+        and positions & (positions - 1) == 0
+        and seq_count & (seq_count - 1) == 0
         and w_out.shape[0] % 64 == 0
         and tokens.shape[3] % (16 * dp_count * seq_count) == 0
         and row_mask.shape[2] == 2
@@ -761,8 +773,8 @@
             pltpu.VMEM((8, z_count, rows, lanes), BF16),
             pltpu.VMEM((8, z_count, rows, lanes), BF16),
             pltpu.VMEM((8, z_count - 1, rows, lanes), BF16),
-            pltpu.SemaphoreType.DMA((5, 4)),
-            pltpu.SemaphoreType.DMA((5, 4)),
+            pltpu.SemaphoreType.DMA((6, 4)),
+            pltpu.SemaphoreType.DMA((6, 4)),
             pltpu.SemaphoreType.DMA((7,)),
             pltpu.SemaphoreType.DMA((7,)),
             pltpu.SemaphoreType.DMA((8, 2 + z_count)),

time: 59.3 us -> 61 us (1.029)
  Pallas kernels: 58.6 us -> 60.3 us
    pallas_call x1, Pallas kernels: 56.4 us -> 58.1 us  [fused_body(): call(tokens.reshape(positions, width), cotangent.reshape(positions, width...]
where the time goes in v6:
time: 61 us; the launch traced here: 60.9 us
  Pallas kernels  60.3 us (99%)
  between operations  0.64 us (1%)
    pallas_call x1, Pallas kernels, fused_body(): call(tokens.reshape(positions, width), cotangent.reshape(positions, width...  58.1 us
    pallas_call x1, Pallas kernels, hand_out(): pl.pallas_call(hand_out_kernel, out_shape=[jax.ShapeDtypeStruct(item.shap...  2.11 us

profile of v6, /device:TPU:0, one launch (start us, length us, event | category | flops | bytes accessed | tf_op | source)
XLA Modules:
  0.0 60.9 jit_solution(3888881139785051541)
XLA Ops:
  0.6 58.1 %shard_map.111 = (bf16[256,1024]{1,0:T(8,128)(2,1)}, bf16[256,1024]{1,0:T(8,128)(2,1)}, f32[32,512]{1,0:T(8,128)}, f32[32,512]{1,0:T(8,128)}) custom-call(bf16[256,1024]{1,0:T(8,128)(2,1)} %bitcast.7, bf16[256,1024]{1,0:T(8,128)(2,1)} %bitcast.8, s32[1,2,2,4]{3,2,1,0:T(2,128)} %bitcast.13, s32[4,2,2,16]{3,2,1,0:T(2,128)} %bitcast.12, ...), custom_call_target="tpu_custom_call" | custom-call | flops 3400000000 | bytes 8000000 | tf_op jit(solution)/shard_map/pallas_call | solution.py:791
  58.8 2.1 %shard_map.112 = (bf16[256,1024]{1,0:T(8,128)(2,1)}, bf16[256,1024]{1,0:T(8,128)(2,1)}, f32[32,512]{1,0:T(8,128)}, f32[32,512]{1,0:T(8,128)}) custom-call(bf16[256,1024]{1,0:T(8,128)(2,1)} %get-tuple-element.12.refs_0_, bf16[256,1024]{1,0:T(8,128)(2,1)} %get-tuple-element.13.refs_1_, f32[32,512]{1,0:T(8,128)} %get-tuple-element.14.refs_2_, ...), custom_call_target="tpu_custom_call" | custom-call | tf_op jit(solution)/shard_map/pallas_call | solution.py:682

commit v7 on v6

--- a/solution.py
+++ b/solution.py
@@ -186,10 +186,6 @@
     return lax.dot_general(a, b, contract_last, preferred_element_type=F32)
 
 
-def dot_tn(a, b):
-    return lax.dot_general(a, b, contract_first, preferred_element_type=F32)
-
-
 def fused_kernel(
     dp_count,
     seq_count,
@@ -212,6 +208,7 @@
     row_mask_ref,
     column_mask_ref,
     bias,
+    unit,
     mixed_ref,
     gtok_ref,
     gval_ref,
@@ -302,6 +299,20 @@
             device_id_type=MESH,
         )
 
+    def store_bias(index, seen):
+        bias[index] = jnp.where(seen, 0.0, -1e30)
+
+    query_pos = lax.broadcasted_iota(jnp.int32, (positions, positions), 0)
+    key_pos = lax.broadcasted_iota(jnp.int32, (positions, positions), 1)
+    differ = query_pos ^ key_pos
+    causal = key_pos <= query_pos
+    matching = causal & ((differ & (cols - 1)) == 0)
+    store_bias(0, causal)
+    store_bias(1, causal & (differ < ROWBLK))
+    store_bias(2, matching)
+    store_bias(3, matching & (differ < COLBLK * cols))
+    unit[...] = jnp.where(differ == 0, 1.0, 0.0).astype(BF16)
+
     for copy in weights_in:
         copy.wait()
     pl.semaphore_wait(barrier, seq_count)
@@ -401,22 +412,12 @@
     first_lanes = lane < HEAD_DIM
     keep = (first_lanes.astype(F32).astype(BF16), (lane >= HEAD_DIM).astype(F32).astype(BF16))
 
-    def store_bias(index, seen):
-        bias[index] = jnp.where(seen, 0.0, -1e30)
-
-    def build_bias():
-        query_pos = lax.broadcasted_iota(jnp.int32, (positions, positions), 0)
-        key_pos = lax.broadcasted_iota(jnp.int32, (positions, positions), 1)
-        differ = query_pos ^ key_pos
-        causal = key_pos <= query_pos
-        matching = causal & ((differ & (cols - 1)) == 0)
-        store_bias(0, causal)
-        store_bias(1, causal & (differ < ROWBLK))
-        store_bias(2, matching)
-        store_bias(3, matching & (differ < COLBLK * cols))
-
     for copy in others_in:
         copy.wait()
+    for first in range(0, tokens_ref.shape[1], positions):
+        block = slice(first, first + positions)
+        tokens_t[block, :] = dot_nt(unit[...], tokens_ref[:, block]).astype(BF16)
+        cot_t[block, :] = dot_nt(unit[...], cot_ref[:, block]).astype(BF16)
 
     def head_bias(head):
         if head < half:
@@ -447,8 +448,11 @@
             outs.append(dot_nn(weights.astype(BF16), value))
         return merge(outs)
 
+    def turned(square):
+        return dot_nt(unit[...], square).astype(BF16)
+
     def value_grad(grad, slot):
-        sides = [dot_tn(probs[slot + side].astype(BF16), grad) for side in range(2)]
+        sides = [dot_nn(turned(probs[slot + side].astype(BF16)), grad) for side in range(2)]
         return merge(sides)
 
     def query_key_grads(query, key, value, grad, slot):
@@ -461,7 +465,7 @@
             )
             grad_scores = (grad_scores * (1.0 / math.sqrt(HEAD_DIM))).astype(BF16)
             grads[0].append(dot_nn(grad_scores, key))
-            grads[1].append(dot_tn(grad_scores, query))
+            grads[1].append(dot_nn(turned(grad_scores), query))
         return [merge(grad_pair) for grad_pair in grads]
 
     def rs_copy(which, hop):
@@ -557,10 +561,7 @@
     weights_here(4)
     g_send[0] = dot_nt(cot_ref[...], wo_full[split:, :]).astype(BF16)
     exchange(g_send, g_recv, 3)
-    build_bias()
     g_rows[...] = dot_nt(cot_ref[...], wo_full[:split, :]).astype(BF16)
-    tokens_t[...] = tokens_ref[...].T
-    cot_t[...] = cot_ref[...].T
     pass_on(5)
 
     for index in range(3):
@@ -701,6 +702,8 @@
         and w_query.shape[0] % 64 == 0
         and w_query.shape[1] % 512 == 0
         and w_out.shape[1] % 256 == 0
+        and tokens.shape[3] % positions == 0
+        and positions % 128 == 0
         and positions & (positions - 1) == 0
         and seq_count & (seq_count - 1) == 0
         and w_out.shape[0] % 64 == 0
@@ -743,6 +746,7 @@
             pltpu.SMEM(stored_row_mask.shape, jnp.int32),
             pltpu.SMEM(stored_column_mask.shape, jnp.int32),
             pltpu.VMEM((4, positions, positions), F32),
+            pltpu.VMEM((positions, positions), BF16),
             pltpu.VMEM((positions, width), BF16),
             pltpu.VMEM((positions, width), BF16),
             pltpu.VMEM((rows, heads_width), F32),

time: 61 us -> 61.4 us (level)
  no operation moved by 1% of the time
where the time goes in v7:
time: 61.4 us; the launch traced here: 61.3 us
  Pallas kernels  60.6 us (99%)
  between operations  0.64 us (1%)
    pallas_call x1, Pallas kernels, fused_body(): call(tokens.reshape(positions, width), cotangent.reshape(positions, width...  58.5 us
    pallas_call x1, Pallas kernels, hand_out(): pl.pallas_call(hand_out_kernel, out_shape=[jax.ShapeDtypeStruct(item.shap...  2.11 us

profile of v7, /device:TPU:0, one launch (start us, length us, event | category | flops | bytes accessed | tf_op | source)
XLA Modules:
  0.0 61.3 jit_solution(9395503385617361936)
XLA Ops:
  0.6 58.5 %shard_map.111 = (bf16[256,1024]{1,0:T(8,128)(2,1)}, bf16[256,1024]{1,0:T(8,128)(2,1)}, f32[32,512]{1,0:T(8,128)}, f32[32,512]{1,0:T(8,128)}) custom-call(bf16[256,1024]{1,0:T(8,128)(2,1)} %bitcast.7, bf16[256,1024]{1,0:T(8,128)(2,1)} %bitcast.8, s32[1,2,2,4]{3,2,1,0:T(2,128)} %bitcast.13, s32[4,2,2,16]{3,2,1,0:T(2,128)} %bitcast.12, ...), custom_call_target="tpu_custom_call" | custom-call | flops 3400000000 | bytes 8000000 | tf_op jit(solution)/shard_map/pallas_call | solution.py:795
  59.2 2.1 %shard_map.112 = (bf16[256,1024]{1,0:T(8,128)(2,1)}, bf16[256,1024]{1,0:T(8,128)(2,1)}, f32[32,512]{1,0:T(8,128)}, f32[32,512]{1,0:T(8,128)}) custom-call(bf16[256,1024]{1,0:T(8,128)(2,1)} %get-tuple-element.12.refs_0_, bf16[256,1024]{1,0:T(8,128)(2,1)} %get-tuple-element.13.refs_1_, f32[32,512]{1,0:T(8,128)} %get-tuple-element.14.refs_2_, ...), custom_call_target="tpu_custom_call" | custom-call | tf_op jit(solution)/shard_map/pallas_call | solution.py:683

commit v8 on v7

--- a/solution.py
+++ b/solution.py
@@ -318,14 +318,13 @@
     pl.semaphore_wait(barrier, seq_count)
 
     def region(group, owner, qy, qc):
-        if group in (3, 4):
+        if group == 3:
             quarter = out_shard // 4
             start = pl.multiple_of(owner * out_shard + (qy * 2 + qc) * quarter, quarter)
-            width = wo_full.shape[1] // 2
-            return wo_full.at[pl.ds(start, quarter), pl.ds((group - 3) * width, width)]
+            return wo_full.at[pl.ds(start, quarter), :]
         quarter = shard // 4
         start = pl.multiple_of(owner * shard + (qy * 2 + qc) * quarter, quarter)
-        if group == 5:
+        if group == 4:
             return w_full.at[:, pl.ds(start, quarter), pl.ds(0, split)]
         return w_full.at[group, pl.ds(start, quarter), pl.ds(split, split)]
 
@@ -349,10 +348,8 @@
 
     def pass_on(group):
         weight_copy(group, 0).wait_recv()
-        if group < 3:
+        if group + 2 < 5:
             weight_copy(group + 2, 0).start()
-        elif group == 4:
-            weight_copy(5, 0).start()
         weight_copy(group, 1).start()
         weight_copy(group, 2).start()
 
@@ -550,27 +547,23 @@
     pass_on(2)
     project_columns(0)
     pass_core(1)
-    pass_on(3)
     project_columns(1)
     pass_core(2)
-    pass_on(4)
+    pass_on(3)
     project_columns(2)
     pass_core(3)
-    pass_core(4)
+    pass_on(4)
     weights_here(3)
-    weights_here(4)
     g_send[0] = dot_nt(cot_ref[...], wo_full[split:, :]).astype(BF16)
     exchange(g_send, g_recv, 3)
     g_rows[...] = dot_nt(cot_ref[...], wo_full[:split, :]).astype(BF16)
-    pass_on(5)
-
     for index in range(3):
         arrived(one(qkv_send, index), one(qkv_recv, index), index)
     for pair in range(split // (2 * HEAD_DIM)):
         query, key, value = (qkv_recv[index, :, pair_of(pair)] for index in range(3))
         out_send[0, :, pair_of(pair)] = forward(half + 2 * pair, query, key, value, 2 * pair)
     exchange(out_send, out_recv, 4)
-    pass_core(5)
+    pass_core(4)
 
     arrived(g_send, g_recv, 3)
     pairs = range(split // (2 * HEAD_DIM))
@@ -584,7 +577,7 @@
             grad_send[index, :, pair_of(pair)] = grads[index]
     exchange(grad_send.at[pl.ds(0, 2)], grad_recv.at[pl.ds(0, 2)], 6)
 
-    weights_here(5)
+    weights_here(4)
     for index in range(3):
         row_qkv[index] = dot_nn(tokens_ref[...], w_full[index, :, :split]).astype(BF16)
     for pair in pairs:
@@ -636,7 +629,7 @@
     outs[1].start()
     rs_next(2, 2)
     rs_next(3, 2)
-    for group in range(6):
+    for group in range(5):
         for hop in range(4):
             weight_copy(group, hop).wait_send()
     for index in range(3):
@@ -777,8 +770,8 @@
             pltpu.VMEM((8, z_count, rows, lanes), BF16),
             pltpu.VMEM((8, z_count, rows, lanes), BF16),
             pltpu.VMEM((8, z_count - 1, rows, lanes), BF16),
-            pltpu.SemaphoreType.DMA((6, 4)),
-            pltpu.SemaphoreType.DMA((6, 4)),
+            pltpu.SemaphoreType.DMA((5, 4)),
+            pltpu.SemaphoreType.DMA((5, 4)),
             pltpu.SemaphoreType.DMA((7,)),
             pltpu.SemaphoreType.DMA((7,)),
             pltpu.SemaphoreType.DMA((8, 2 + z_count)),

time: 61.4 us -> 59.9 us (0.976)
  Pallas kernels: 60.6 us -> 59.1 us
    pallas_call x1, Pallas kernels: 58.5 us -> 57 us  [fused_body(): call(tokens.reshape(positions, width), cotangent.reshape(positions, width...]
where the time goes in v8:
time: 59.9 us; the launch traced here: 59.7 us
  Pallas kernels  59.1 us (99%)
  between operations  0.64 us (1%)
    pallas_call x1, Pallas kernels, fused_body(): call(tokens.reshape(positions, width), cotangent.reshape(positions, width...  57 us
    pallas_call x1, Pallas kernels, hand_out(): pl.pallas_call(hand_out_kernel, out_shape=[jax.ShapeDtypeStruct(item.shap...  2.11 us

profile of v8, /device:TPU:0, one launch (start us, length us, event | category | flops | bytes accessed | tf_op | source)
XLA Modules:
  0.0 59.7 jit_solution(1187814446706540118)
XLA Ops:
  0.6 57.0 %shard_map.111 = (bf16[256,1024]{1,0:T(8,128)(2,1)}, bf16[256,1024]{1,0:T(8,128)(2,1)}, f32[32,512]{1,0:T(8,128)}, f32[32,512]{1,0:T(8,128)}) custom-call(bf16[256,1024]{1,0:T(8,128)(2,1)} %bitcast.7, bf16[256,1024]{1,0:T(8,128)(2,1)} %bitcast.8, s32[1,2,2,4]{3,2,1,0:T(2,128)} %bitcast.13, s32[4,2,2,16]{3,2,1,0:T(2,128)} %bitcast.12, ...), custom_call_target="tpu_custom_call" | custom-call | flops 3400000000 | bytes 8000000 | tf_op jit(solution)/shard_map/pallas_call | solution.py:788
  57.6 2.1 %shard_map.112 = (bf16[256,1024]{1,0:T(8,128)(2,1)}, bf16[256,1024]{1,0:T(8,128)(2,1)}, f32[32,512]{1,0:T(8,128)}, f32[32,512]{1,0:T(8,128)}) custom-call(bf16[256,1024]{1,0:T(8,128)(2,1)} %get-tuple-element.12.refs_0_, bf16[256,1024]{1,0:T(8,128)(2,1)} %get-tuple-element.13.refs_1_, f32[32,512]{1,0:T(8,128)} %get-tuple-element.14.refs_2_, ...), custom_call_target="tpu_custom_call" | custom-call | tf_op jit(solution)/shard_map/pallas_call | solution.py:676
